TPU v7x, 32 devices: a whole 2x2x4 slice. The times are simulated.
32 devices in a mesh: blk: 8 (over y, x, core), tp: 4 (over z).
Axes of the slice: x: 2, y: 2, z: 4, core: 2. Of those that a mesh axis runs over, the one named last changes fastest.
Arguments:
- hidden_in: bfloat16 [4096, 1536], P('blk'), may hold values from -6 to 6
- out_grad: bfloat16 [4096, 1536], P('blk'), may hold values from -6 to 6
- lengths: int32 [5], replicated, may hold values from 1 to 2560, as said below
- attn_gain: float32 [1536], replicated, may hold values from 0.5 to 1.5
- w_query: bfloat16 [1536, 1536], P(None, 'tp'), may hold values from -0.15625 to 0.15625
- key_projection_weight: bfloat16 [1536, 768], P(None, 'tp'), may hold values from -0.15625 to 0.15625
- value_projection_weight: bfloat16 [1536, 768], P(None, 'tp'), may hold values from -0.15625 to 0.15625
- w_out: bfloat16 [1536, 1536], P('tp'), may hold values from -6 to 6
- mlp_gain: float32 [1536], replicated, may hold values from 0.5 to 1.5
- w_gate: bfloat16 [1536, 4096], P(None, 'tp'), may hold values from -0.15625 to 0.15625
- w_up: bfloat16 [1536, 4096], P(None, 'tp'), may hold values from -0.15625 to 0.15625
- w_down: bfloat16 [4096, 1536], P('tp'), may hold values from -0.375 to 0.375
Outputs:
- layer_out: bfloat16 [4096, 1536], P('blk')
- input_grad: bfloat16 [4096, 1536], P('blk')
- grad_query: float32 [1536, 1536], P('blk', 'tp')
- grad_key: float32 [1536, 768], P('blk', 'tp')
- grad_value: float32 [1536, 768], P('blk', 'tp')
- grad_out: float32 [1536, 1536], P('tp', 'blk')
- grad_gate: float32 [1536, 4096], P('blk', 'tp')
- grad_up: float32 [1536, 4096], P('blk', 'tp')
- grad_down: float32 [4096, 1536], P('tp', 'blk')
- grad_attn_gain: float32 [1536], P('blk')
- grad_mlp_gain: float32 [1536], P('blk')
Inputs may be any that keep to these rules, and one draw needn't show every extreme that they name: The lengths sum to 4096. The first entry is a piece of 1 to min(512, 512) - 1 tokens drawn from the seed and the last entry is 512 minus it; of the entries between, exactly one, at a place drawn from the seed, is 2560 and all others are 512.
All inputs are finite; a program needn't handle non-finite values.
Results may differ from a plain program's by a relative error of at most 0.03.
Values may be sent and summed in bfloat16 or wider, within the bound.
A program may use at most 192 MiB of HBM per device.

v0:
```python
import jax
import jax.numpy as jnp
from jax import lax
from jax.sharding import PartitionSpec as P

HEAD_SIZE = 96


norm_eps = 1e-05
rope_base = 100000.0
neg_fill = -1e30


def doc_places(lengths, places):
    doc_ends = jnp.cumsum(lengths)
    passed = (places[:, None] >= doc_ends[None, :]).astype(jnp.int32)
    segment = jnp.sum(passed, axis=1)
    preceding = jnp.sum(passed * lengths[None, :], axis=1)
    return (segment, places - preceding)


def apply_rotary(values, token_position, heads, sign_value):
    half_size = HEAD_SIZE // 2
    freqs = rope_base ** (-(2.0 * jnp.arange(half_size, dtype=jnp.float32)) / HEAD_SIZE)
    angle = token_position.astype(jnp.float32)[:, None] * freqs[None, :]
    cosine = jnp.cos(angle)[:, None, :]
    sine = sign_value * jnp.sin(angle)[:, None, :]
    shaped = values.reshape(values.shape[0], heads, HEAD_SIZE)
    first_half = shaped[..., :half_size]
    second_half = shaped[..., half_size:]
    turned = jnp.concatenate(
        [first_half * cosine - second_half * sine, second_half * cosine + first_half * sine],
        axis=-1,
    )
    return turned.reshape(values.shape[0], heads * HEAD_SIZE)


def rms_parts(values):
    inverse = lax.rsqrt(jnp.mean(values * values, axis=-1, keepdims=True) + norm_eps)
    return (values * inverse, inverse)


def norm_back(grad_in, normed, inverse, gain):
    scaled = grad_in * gain
    grad_values = inverse * (scaled - normed * jnp.mean(scaled * normed, axis=-1, keepdims=True))
    return (grad_values, jnp.sum(grad_in * normed, axis=0))


def left_product(left_side, right_side):
    return lax.dot_general(
        left_side, right_side, (((0,), (0,)), ((), ())), preferred_element_type=jnp.float32
    )


def right_product(left_side, weight):
    return lax.dot_general(
        left_side, weight, (((1,), (1,)), ((), ())), preferred_element_type=jnp.float32
    )


def score_block(query_four, key_rows, query_seg, query_place, key_seg, key_place):
    score_scale = HEAD_SIZE ** (-0.5)
    scores = (
        jnp.einsum("igrd,jgd->grij", query_four, key_rows, preferred_element_type=jnp.float32)
        * score_scale
    )
    allowed = (query_seg[:, None] == key_seg[None, :]) & (
        key_place[None, :] <= query_place[:, None]
    )
    return (jnp.where(allowed[None, None], scores, neg_fill), allowed)


def score_grads(
    query_four,
    grad_four,
    log_sum,
    delta,
    query_seg,
    query_place,
    key_rows,
    value_rows,
    key_seg,
    key_place,
):
    scores, allowed = score_block(query_four, key_rows, query_seg, query_place, key_seg, key_place)
    probs = jnp.where(allowed[None, None], jnp.exp(scores - log_sum[..., None]), 0.0)
    grad_probs = jnp.einsum(
        "igrd,jgd->grij", grad_four, value_rows, preferred_element_type=jnp.float32
    )
    grad_scores = (probs * (grad_probs - delta[..., None])).astype(jnp.bfloat16)
    return (grad_scores, probs.astype(jnp.bfloat16))


def keep_same(running):
    return running


def shards(
    hidden_in,
    out_grad,
    lengths,
    attn_gain,
    w_query,
    key_projection_weight,
    value_projection_weight,
    w_out,
    mlp_gain,
    w_gate,
    w_up,
    w_down,
):
    row_count = hidden_in.shape[0]
    cycle_size = lax.axis_size("blk")
    first_row = lax.axis_index("blk") * row_count
    offsets = jnp.arange(row_count, dtype=jnp.int32)
    places = first_row + offsets
    segment, token_position = doc_places(lengths, places)
    q_heads = w_query.shape[1] // HEAD_SIZE
    kv_heads = key_projection_weight.shape[1] // HEAD_SIZE
    query_group_size = q_heads // kv_heads
    kv_width = kv_heads * HEAD_SIZE
    score_scale = HEAD_SIZE ** (-0.5)
    hidden_f = hidden_in.astype(jnp.float32)
    normed_one, inverse_one = rms_parts(hidden_f)
    first_layer_norm = (normed_one * attn_gain).astype(jnp.bfloat16)
    query_raw = jnp.dot(first_layer_norm, w_query, preferred_element_type=jnp.float32)
    key_raw = jnp.dot(first_layer_norm, key_projection_weight, preferred_element_type=jnp.float32)
    value_raw = jnp.dot(
        first_layer_norm, value_projection_weight, preferred_element_type=jnp.float32
    )
    query_low = apply_rotary(query_raw, token_position, q_heads, 1.0).astype(jnp.bfloat16)
    key_low = apply_rotary(key_raw, token_position, kv_heads, 1.0).astype(jnp.bfloat16)
    value_low = value_raw.astype(jnp.bfloat16)
    kv_rows = jnp.concatenate([key_low, value_low], axis=1)
    query_four = query_low.reshape(row_count, kv_heads, query_group_size, HEAD_SIZE)

    def split_kv(piece, block_step):
        block_rows = lax.dynamic_slice_in_dim(piece, block_step * row_count, row_count, 0)
        key_rows = block_rows[:, :kv_width].reshape(row_count, kv_heads, HEAD_SIZE)
        value_rows = block_rows[:, kv_width:].reshape(row_count, kv_heads, HEAD_SIZE)
        return (key_rows, value_rows)

    start_max = jnp.full((kv_heads, query_group_size, row_count), neg_fill, jnp.float32)
    start_sum = jnp.zeros((kv_heads, query_group_size, row_count), jnp.float32)
    start_acc = jnp.zeros((kv_heads, query_group_size, row_count, HEAD_SIZE), jnp.float32)
    piece = lax.all_gather(kv_rows, "blk", axis=0, tiled=True)

    def forward_one_step(block_step, running):
        key_start = block_step * row_count

        def forward_work(running):
            row_max, row_sum, weighted = running
            key_rows, value_rows = split_kv(piece, block_step)
            key_place = key_start + offsets
            key_seg, _ = doc_places(lengths, key_place)
            scores, allowed = score_block(query_four, key_rows, segment, places, key_seg, key_place)
            new_max = jnp.maximum(row_max, jnp.max(scores, axis=-1))
            exp_scores = jnp.where(allowed[None, None], jnp.exp(scores - new_max[..., None]), 0.0)
            rescale = jnp.exp(row_max - new_max)
            row_sum = row_sum * rescale + jnp.sum(exp_scores, axis=-1)
            weighted = weighted * rescale[..., None] + jnp.einsum(
                "grij,jgd->grid",
                exp_scores.astype(jnp.bfloat16),
                value_rows,
                preferred_element_type=jnp.float32,
            )
            return (new_max, row_sum, weighted)

        return lax.cond(key_start <= first_row, forward_work, keep_same, running)

    row_max, row_sum, weighted = lax.fori_loop(
        0, piece.shape[0] // row_count, forward_one_step, (start_max, start_sum, start_acc)
    )
    attn_four = weighted / row_sum[..., None]
    log_sum = row_max + jnp.log(row_sum)
    attn_rows = jnp.transpose(attn_four, (2, 0, 1, 3)).reshape(row_count, q_heads * HEAD_SIZE)
    attn_low = attn_rows.astype(jnp.bfloat16)
    branch = lax.psum(jnp.dot(attn_low, w_out, preferred_element_type=jnp.float32), "tp")
    middle = hidden_f + branch
    normed_two, inverse_two = rms_parts(middle)
    ln_two = (normed_two * mlp_gain).astype(jnp.bfloat16)
    gate = jnp.dot(ln_two, w_gate, preferred_element_type=jnp.float32)
    up_proj = jnp.dot(ln_two, w_up, preferred_element_type=jnp.float32)
    sig_gate = jax.nn.sigmoid(gate)
    act_gate = gate * sig_gate
    hidden = (act_gate * up_proj).astype(jnp.bfloat16)
    mlp_branch = lax.psum(jnp.dot(hidden, w_down, preferred_element_type=jnp.float32), "tp")
    layer_out = (middle + mlp_branch).astype(jnp.bfloat16)
    grad_down = left_product(hidden, out_grad)
    grad_hidden = right_product(out_grad, w_down)
    grad_gate_act = (grad_hidden * up_proj * sig_gate * (1.0 + gate * (1.0 - sig_gate))).astype(
        jnp.bfloat16
    )
    grad_up_act = (grad_hidden * act_gate).astype(jnp.bfloat16)
    grad_gate = left_product(ln_two, grad_gate_act)
    grad_up = left_product(ln_two, grad_up_act)
    grad_ln_two = lax.psum(
        right_product(grad_gate_act, w_gate) + right_product(grad_up_act, w_up), "tp"
    )
    grad_middle_norm, grad_mlp_gain = norm_back(grad_ln_two, normed_two, inverse_two, mlp_gain)
    grad_middle = out_grad.astype(jnp.float32) + grad_middle_norm
    grad_branch = grad_middle.astype(jnp.bfloat16)
    grad_out = left_product(attn_low, grad_branch)
    grad_attn = right_product(grad_branch, w_out).astype(jnp.bfloat16)
    grad_four = grad_attn.reshape(row_count, kv_heads, query_group_size, HEAD_SIZE)
    delta = jnp.sum(jnp.transpose(grad_four.astype(jnp.float32), (1, 2, 0, 3)) * attn_four, axis=-1)

    def query_grads(grad_scores, key_rows):
        return (
            jnp.einsum("grij,jgd->grid", grad_scores, key_rows, preferred_element_type=jnp.float32)
            * score_scale
        )

    def key_value_grads(grad_scores, probs_low, query_rows, grad_rows):
        grad_keys = (
            jnp.einsum(
                "grij,igrd->jgd", grad_scores, query_rows, preferred_element_type=jnp.float32
            )
            * score_scale
        )
        grad_values = jnp.einsum(
            "grij,igrd->jgd", probs_low, grad_rows, preferred_element_type=jnp.float32
        )
        return jnp.concatenate(
            [grad_keys.reshape(row_count, kv_width), grad_values.reshape(row_count, kv_width)],
            axis=1,
        )

    start_dq = jnp.zeros((kv_heads, query_group_size, row_count, HEAD_SIZE), jnp.float32)
    start_kv = jnp.zeros((row_count * cycle_size, 2 * kv_width), jnp.float32)
    back_piece = lax.all_gather(kv_rows, "blk", axis=0, tiled=True)

    def back_one_step(block_step, running):
        key_start = block_step * row_count

        def back_work(running):
            grad_query_acc, grad_kv_acc = running
            key_rows, value_rows = split_kv(back_piece, block_step)
            key_place = key_start + offsets
            key_seg, _ = doc_places(lengths, key_place)
            grad_scores, probs_low = score_grads(
                query_four,
                grad_four,
                log_sum,
                delta,
                segment,
                places,
                key_rows,
                value_rows,
                key_seg,
                key_place,
            )
            grad_query_acc = grad_query_acc + query_grads(grad_scores, key_rows)
            earlier = lax.dynamic_slice_in_dim(grad_kv_acc, key_start, row_count, 0)
            added = earlier + key_value_grads(grad_scores, probs_low, query_four, grad_four)
            return (
                grad_query_acc,
                lax.dynamic_update_slice_in_dim(grad_kv_acc, added, key_start, 0),
            )

        return lax.cond(key_start <= first_row, back_work, keep_same, running)

    grad_query_four, grad_kv_all = lax.fori_loop(
        0, back_piece.shape[0] // row_count, back_one_step, (start_dq, start_kv)
    )
    grad_kv = lax.psum_scatter(grad_kv_all, "blk", scatter_dimension=0, tiled=True)
    grad_query_rows = jnp.transpose(grad_query_four, (2, 0, 1, 3)).reshape(
        row_count, q_heads * HEAD_SIZE
    )
    grad_query_low = apply_rotary(grad_query_rows, token_position, q_heads, -1.0).astype(
        jnp.bfloat16
    )
    grad_key_low = apply_rotary(grad_kv[:, :kv_width], token_position, kv_heads, -1.0).astype(
        jnp.bfloat16
    )
    grad_value_low = grad_kv[:, kv_width:].astype(jnp.bfloat16)
    grad_query = left_product(first_layer_norm, grad_query_low)
    grad_key = left_product(first_layer_norm, grad_key_low)
    grad_value = left_product(first_layer_norm, grad_value_low)
    grad_ln_part = (
        right_product(grad_query_low, w_query)
        + right_product(grad_key_low, key_projection_weight)
        + right_product(grad_value_low, value_projection_weight)
    )
    grad_ln_one = lax.psum(grad_ln_part, "tp")
    grad_input_norm, grad_attn_gain = norm_back(grad_ln_one, normed_one, inverse_one, attn_gain)
    input_grad = (grad_middle + grad_input_norm).astype(jnp.bfloat16)
    summed = (
        lax.psum_scatter(grad_query, "blk", scatter_dimension=0, tiled=True),
        lax.psum_scatter(grad_key, "blk", scatter_dimension=0, tiled=True),
        lax.psum_scatter(grad_value, "blk", scatter_dimension=0, tiled=True),
        lax.psum_scatter(grad_out, "blk", scatter_dimension=1, tiled=True),
        lax.psum_scatter(grad_gate, "blk", scatter_dimension=0, tiled=True),
        lax.psum_scatter(grad_up, "blk", scatter_dimension=0, tiled=True),
        lax.psum_scatter(grad_down, "blk", scatter_dimension=1, tiled=True),
        lax.psum_scatter(grad_attn_gain, "blk", scatter_dimension=0, tiled=True),
        lax.psum_scatter(grad_mlp_gain, "blk", scatter_dimension=0, tiled=True),
    )
    return (
        layer_out,
        input_grad,
        summed[0],
        summed[1],
        summed[2],
        summed[3],
        summed[4],
        summed[5],
        summed[6],
        summed[7],
        summed[8],
    )


def solution(mesh):
    placed = (
        P("blk", None),
        P("blk", None),
        P(),
        P(),
        P(None, "tp"),
        P(None, "tp"),
        P(None, "tp"),
        P("tp", None),
        P(),
        P(None, "tp"),
        P(None, "tp"),
        P("tp", None),
    )
    return jax.shard_map(
        shards,
        mesh=mesh,
        in_specs=placed,
        out_specs=(
            P("blk", None),
            P("blk", None),
            P("blk", "tp"),
            P("blk", "tp"),
            P("blk", "tp"),
            P("tp", "blk"),
            P("blk", "tp"),
            P("blk", "tp"),
            P("tp", "blk"),
            P("blk"),
            P("blk"),
        ),
        check_vma=False,
    )
```

profile of v0, /device:TPU:0, one launch (start us, length us, event | category | flops | bytes accessed | tf_op | source)
XLA Modules:
  0.0 1168.3 jit_solution(12842330488488591940)
XLA Ops:
  19.5 32.8 %all-gather.2.cloned.1.call-done = bf16[4096,384]{0,1:T(8,128)(2,1)} async-done(((bf16[512,384]{0,1:T(8,128)(2,1)}), bf16[4096,384]{0,1:T(8,128)(2,1)}) %all-gather.2.cloned.1.call-update) | async-done | bytes 3145744 | tf_op jit(solution)/shard_map/all_gather | solution.py:146
  53.3 14.0 %while.36 = (s32[]{:T(128)}, f32[2,2,512]{2,1,0:T(2,128)S(1)}, f32[2,2,512]{2,1,0:T(2,128)S(1)}, f32[2,2,512,96]{2,3,1,0:T(8,128)}, s32[]{:T(128)}, /*index=5*/s...) while((s32[]{:T(128)}, f32[2,2,512]{2,1,0:T(2,128)S(1)}, ...), condition=%wide.region_11.12_spmd.clone.clone, body=%wide.region_4.11_spmd.clone.clone.sunk | while | flops 417476640 | bytes 23222760 | solution.py:171
  53.8 9.3 conditional.8
  69.2 3.9 fusion.69
  73.4 186.1 %all-reduce.8.cloned.1.call-done = f32[512,1536]{1,0:T(8,128)} async-done(((f32[512,1536]{1,0:T(8,128)}), f32[512,1536]{1,0:T(8,128)}) %all-reduce.8.cloned.1.call-update) | async-done | bytes 3145744 | tf_op jit(solution)/shard_map/psum | solution.py:178
  269.7 3.5 multiply_convert_fusion.1
  275.0 3.5 convolution_add_fusion.2
  279.5 119.4 %all-reduce.10.cloned.1.call-done = f32[512,1536]{1,0:T(8,128)} async-done(((f32[512,1536]{1,0:T(8,128)}), f32[512,1536]{1,0:T(8,128)}) %all-reduce.10.cloned.1.call-update) | async-done | bytes 3145744 | tf_op jit(solution)/shard_map/psum | solution.py:197
  398.9 4.3 multiply_reduce_fusion
  409.5 3.4 broadcast_in_dim.50
  412.9 10.8 while.37
  412.9 10.5 conditional.9
  423.8 4.8 fusion.72
  432.3 124.7 %reduce-scatter.9.cloned.1.call-done = f32[512,384]{0,1:T(8,128)} async-done(((f32[4096,384]{0,1:T(8,128)}), f32[512,384]{0,1:T(8,128)}) %reduce-scatter.9.cloned.1.call-update) | async-done | bytes 786448 | tf_op jit(solution)/shard_map/reduce_scatter | solution.py:266
  564.2 4.3 fusion.49
  568.6 4.6 fusion.59
  573.3 6.2 fusion.77
  579.6 6.2 fusion.76
  585.8 6.1 fusion.75
  592.9 3.4 fusion.57
  596.3 3.4 fusion.53
  601.0 185.7 %all-reduce.12.cloned.1.call-done = (f32[512,1536]{1,0:T(8,128)}, f32[512,1536]{1,0:T(8,128)}) async-done(((f32[512,1536]{1,0:T(8,128)}, f32[512,1536]{1,0:T(8,128)}), (f32[512,1536]{1,0:T(8,128)}, f32[512,1536]{1,0:T(8,128)})) %all-reduce.12.cloned.1.call-update) | async-done | bytes 6291472 | tf_op jit(solution)/shard_map/psum | solution.py:187
  786.6 3.2 fusion.45
  789.8 24.1 %all-reduce.2 = (f32[1536]{0:T(1024)S(1)}, f32[1536]{0:T(1024)S(1)}) all-reduce(f32[1536]{0:T(1024)S(1)} %get-tuple-element.634, f32[1536]{0:T(1024)S(1)} %copy-done.36), channel_id=10, replica_groups=mesh['blk'=8,'tp'=4] {'blk'}, use_global_device_ids=true, to_apply=%region_35.36.clone | all-reduce | flops 3072 | bytes 24576
  815.3 7.8 fusion.44
  823.0 9.2 reduce-scatter.17.cloned.1.call-done
  832.3 46.4 %reduce-scatter.11.cloned.1.call-done = f32[192,384]{1,0:T(8,128)} async-done(((f32[1536,384]{1,0:T(8,128)}), f32[192,384]{1,0:T(8,128)}) %reduce-scatter.11.cloned.1.call-update) | async-done | bytes 294928 | tf_op jit(solution)/shard_map/reduce_scatter | solution.py:289
  878.7 66.1 %reduce-scatter.23.cloned.1.call-done = f32[1024,192]{0,1:T(8,128)} async-done(((f32[1024,1536]{0,1:T(8,128)}), f32[1024,192]{0,1:T(8,128)}) %reduce-scatter.23.cloned.1.call-update) | async-done | bytes 786448 | tf_op jit(solution)/shard_map/reduce_scatter | solution.py:295
  944.8 65.7 %reduce-scatter.21.cloned.1.call-done = f32[192,1024]{1,0:T(8,128)} async-done(((f32[1536,1024]{1,0:T(8,128)}), f32[192,1024]{1,0:T(8,128)}) %reduce-scatter.21.cloned.1.call-update) | async-done | bytes 786448 | tf_op jit(solution)/shard_map/reduce_scatter | solution.py:294
  1010.5 65.9 %reduce-scatter.19.cloned.1.call-done = f32[192,1024]{1,0:T(8,128)} async-done(((f32[1536,1024]{1,0:T(8,128)}), f32[192,1024]{1,0:T(8,128)}) %reduce-scatter.19.cloned.1.call-update) | async-done | bytes 786448 | tf_op jit(solution)/shard_map/reduce_scatter | solution.py:293
  1076.5 42.3 %reduce-scatter.13.cloned.1.call-done = f32[192,192]{1,0:T(8,128)} async-done(((f32[1536,192]{1,0:T(8,128)}), f32[192,192]{1,0:T(8,128)}) %reduce-scatter.13.cloned.1.call-update) | async-done | bytes 147472 | tf_op jit(solution)/shard_map/reduce_scatter | solution.py:290
  1118.8 42.2 %reduce-scatter.15.cloned.1.call-done = f32[192,192]{1,0:T(8,128)} async-done(((f32[1536,192]{1,0:T(8,128)}), f32[192,192]{1,0:T(8,128)}) %reduce-scatter.15.cloned.1.call-update) | async-done | bytes 147472 | tf_op jit(solution)/shard_map/reduce_scatter | solution.py:291
  (212 shorter events, 72.7 us)
Async XLA Ops:
  7.2 262.5 %copy-start = (bf16[1024,1536]{1,0:T(8,128)(2,1)S(1)}, bf16[1024,1536]{1,0:T(8,128)(2,1)}, u32[]{:S(2)}) copy-start(bf16[1024,1536]{1,0:T(8,128)(2,1)} %param.31) | copy-start | bytes 9437188
  7.2 6.7 copy-start.32
  7.2 45.1 %all-gather.2.cloned.1.call-start = ((), (), s32[]{:S(2)}) async-start(), calls=%async_computation.8 | async-start | bytes 3538944 | tf_op jit(solution)/shard_map/all_gather | solution.py:146
  9.2 7.4 copy-start.37
  10.1 3.8 copy-start.7
  10.1 3.8 copy-start.27
  15.7 3.6 copy-start.15
  16.6 242.9 %all-reduce.8.cloned.1.call-start = ((), (), s32[]{:S(2)}) async-start(), calls=%async_computation.9 | async-start | bytes 6291456 | tf_op jit(solution)/shard_map/psum | solution.py:178
  73.2 325.7 %all-reduce.10.cloned.1.call-start = ((), (), s32[]{:S(2)}) async-start(), calls=%async_computation.10 | async-start | bytes 6291456 | tf_op jit(solution)/shard_map/psum | solution.py:197
  262.3 4.8 copy-start.1
  262.4 4.8 copy-start.34
  278.6 278.3 %reduce-scatter.9.cloned.1.call-start = ((), (), s32[]{:S(2)}) async-start(), calls=%async_computation.11 | async-start | bytes 7077888 | tf_op jit(solution)/shard_map/reduce_scatter | solution.py:266
  279.5 123.7 %copy-start.31 = (f32[1536]{0:T(1024)S(1)}, f32[1536]{0:T(1024)}, u32[]{:S(2)}) copy-start(f32[1536]{0:T(1024)} %param.28) | copy-start | bytes 18436
  398.9 4.4 copy-start.2
  398.9 4.7 copy-start.8
  398.9 4.7 copy-start.35
  406.9 6.0 copy-start.17
  423.7 362.9 %all-reduce.12.cloned.1.call-start = ((), (), s32[]{:S(2)}) async-start(), calls=%async_computation.19 | async-start | bytes 12582912 | tf_op jit(solution)/shard_map/psum | solution.py:187
  423.8 4.8 copy-start.6
  423.8 4.8 copy-start.16
  423.8 4.8 copy-start.23
  423.8 5.7 copy-start.22
  563.3 5.3 copy-start.33
  563.3 5.3 copy-start.38
  563.3 269.0 %reduce-scatter.17.cloned.1.call-start = ((), (), s32[]{:S(2)}) async-start(), calls=%async_computation.15 | async-start | bytes 2654208 | tf_op jit(solution)/shard_map/reduce_scatter | solution.py:292
  568.6 310.2 %reduce-scatter.11.cloned.1.call-start = ((), (), s32[]{:S(2)}) async-start(), calls=%async_computation.12 | async-start | bytes 2654208 | tf_op jit(solution)/shard_map/reduce_scatter | solution.py:289
  573.3 371.5 %reduce-scatter.23.cloned.1.call-start = ((), (), s32[]{:S(2)}) async-start(), calls=%async_computation.18 | async-start | bytes 7077888 | tf_op jit(solution)/shard_map/reduce_scatter | solution.py:295
  579.5 431.0 %reduce-scatter.21.cloned.1.call-start = ((), (), s32[]{:S(2)}) async-start(), calls=%async_computation.17 | async-start | bytes 7077888 | tf_op jit(solution)/shard_map/reduce_scatter | solution.py:294
  585.8 490.7 %reduce-scatter.19.cloned.1.call-start = ((), (), s32[]{:S(2)}) async-start(), calls=%async_computation.16 | async-start | bytes 7077888 | tf_op jit(solution)/shard_map/reduce_scatter | solution.py:293
  592.0 526.9 %reduce-scatter.13.cloned.1.call-start = ((), (), s32[]{:S(2)}) async-start(), calls=%async_computation.13 | async-start | bytes 1769472 | tf_op jit(solution)/shard_map/reduce_scatter | solution.py:290
  596.3 564.8 %reduce-scatter.15.cloned.1.call-start = ((), (), s32[]{:S(2)}) async-start(), calls=%async_computation.14 | async-start | bytes 1769472 | tf_op jit(solution)/shard_map/reduce_scatter | solution.py:291
  599.7 190.2 %copy-start.36 = (f32[1536]{0:T(1024)S(1)}, f32[1536]{0:T(1024)}, u32[]{:S(2)}) copy-start(f32[1536]{0:T(1024)} %get-tuple-element.632) | copy-start | bytes 18436
  (26 other events, 53.7 us)
Sparse Core Ops, SparseCore 0:
  16.7 35.5 all-gather.1
  73.3 186.1 all-reduce.7
  278.7 120.0 all-reduce.9
  423.8 133.0 reduce-scatter.8
  563.4 223.1 all-reduce.11
  790.8 41.4 reduce-scatter.16
  836.2 42.4 reduce-scatter.10
  883.0 61.7 reduce-scatter.22
  948.8 61.7 reduce-scatter.20
  1014.7 61.7 reduce-scatter.18
  1080.4 38.4 reduce-scatter.12
  1122.5 38.4 reduce-scatter.14
where the time goes:
time: 1180 us; the launch traced here: 1170 us
  waiting for transfers between devices  987 us (84%)
  matrix products  77.4 us (7%)
  other arithmetic  38.7 us (3%)
  blocking collectives  24.1 us (2%)
  local copies, waits for them, and re-layouts  24 us (2%)
  between operations  15.8 us (1%)
    psum x1, waiting for transfers between devices, shards(): lax.psum(jnp.dot(attn_low, w_out, preferred_element_type=jnp.float32), 'tp')  186 us
    psum x1, waiting for transfers between devices, shards(): lax.psum(jnp.dot(hidden, w_down, preferred_element_type=jnp.float32), 'tp')  186 us
    reduce_scatter x1, waiting for transfers between devices, shards(): lax.psum_scatter(grad_kv_all, 'blk', scatter_dimension=0, tiled=True)  125 us
    psum x1, waiting for transfers between devices, shards(): lax.psum(right_product(grad_gate_act, w_gate) + right_product(grad_up_act...  119 us
    reduce_scatter x1, waiting for transfers between devices, shards(): lax.psum_scatter(grad_down, 'blk', scatter_dimension=1, tiled=True)  66.1 us
    reduce_scatter x1, waiting for transfers between devices, shards(): lax.psum_scatter(grad_gate, 'blk', scatter_dimension=0, tiled=True)  65.9 us
    reduce_scatter x1, waiting for transfers between devices, shards(): lax.psum_scatter(grad_up, 'blk', scatter_dimension=0, tiled=True)  65.7 us
    reduce_scatter x1, waiting for transfers between devices, shards(): lax.psum_scatter(grad_query, 'blk', scatter_dimension=0, tiled=True)  46.4 us
  transfers between devices with their start and end apart: 12, of which 12 were waited for; matrix products, arithmetic and copies ran while one was open for 5% of the time, Pallas kernels for 0%

commit v1 on v0

--- a/solution.py
+++ b/solution.py
@@ -1,6 +1,10 @@
+import functools
+
 import jax
 import jax.numpy as jnp
 from jax import lax
+from jax.experimental import pallas as pl
+from jax.experimental.pallas import tpu as pltpu
 from jax.sharding import PartitionSpec as P
 
 HEAD_SIZE = 96
@@ -311,7 +315,752 @@
     )
 
 
+MESH = pl.DeviceIdType.MESH
+F32, BF16 = jnp.float32, jnp.bfloat16
+LOG2E = 1.4426950408889634
+SCORE_SCALE = HEAD_SIZE**-0.5
+VMEM_BYTES = 62 * 2**20
+HALF = HEAD_SIZE // 2
+
+
+def dot_nn(a, b):
+    return lax.dot_general(a, b, (((1,), (0,)), ((), ())), preferred_element_type=F32)
+
+
+def dot_nt(a, b):
+    return lax.dot_general(a, b, (((1,), (1,)), ((), ())), preferred_element_type=F32)
+
+
+def dot_tn(a, b):
+    return lax.dot_general(a, b, (((0,), (0,)), ((), ())), preferred_element_type=F32)
+
+
+class Place:
+    def __init__(self):
+        self.b = lax.axis_index("blk")
+        self.t = lax.axis_index("tp")
+        self.core = self.b % 2
+        self.chip = self.b // 2
+        self.x = self.chip % 2
+        self.y = self.b // 4
+        self.mate = self.b + 1 - 2 * self.core
+        self.inner = jnp.logical_or(self.t == 1, self.t == 2)
+        self.outer = jnp.logical_not(self.inner)
+        self.pair = self.t + 1 - 2 * (self.t % 2)
+        self.across = 3 - self.t
+
+    def slot(self, s):
+        core = (self.core + s % 2) % 2
+        x = (self.x + (s // 2) % 2) % 2
+        y = (self.y + s // 4) % 2
+        return (y * 2 + x) * 2 + core
+
+    def chip_at(self, k):
+        x = (self.x + (k + 1) % 2) % 2
+        y = (self.y + 1 - k // 2) % 2
+        return y * 2 + x
+
+
+def remote(src, dst, ssem, rsem, b, t):
+    return pltpu.make_async_remote_copy(
+        src_ref=src, dst_ref=dst, send_sem=ssem, recv_sem=rsem, device_id=(b, t), device_id_type=MESH
+    )
+
+
+def enter(me, blk_steps):
+    barrier = pltpu.get_barrier_semaphore()
+    for s in blk_steps:
+        pl.semaphore_signal(barrier, inc=1, device_id=(me.slot(s), me.t), device_id_type=MESH)
+    for z in (me.pair, me.across):
+        pl.semaphore_signal(barrier, inc=1, device_id=(me.b, z), device_id_type=MESH)
+    pl.semaphore_wait(barrier, len(blk_steps) + 2)
+
+
+class LineSum:
+    def __init__(self, me, part, first, second, sems, rows):
+        self.me, self.part, self.first, self.second, self.sems, self.rows = (
+            me, part, first, second, sems, rows,
+        )
+
+    def at(self, ref, p):
+        return ref.at[pl.ds(pl.multiple_of(p * self.rows, self.rows), self.rows), :]
+
+    def copy(self, stage, p):
+        me = self.me
+        src = (self.part, self.part, self.first)[stage]
+        dst = (self.first, self.second, self.first)[stage]
+        target = (me.pair, me.across, me.pair)[stage]
+        return remote(
+            self.at(src, p), self.at(dst, p),
+            self.sems.at[2 * stage, p], self.sems.at[2 * stage + 1, p], me.b, target,
+        )
+
+    def give(self, p):
+        @pl.when(self.me.outer)
+        def _():
+            self.copy(0, p).start()
+
+    def fold(self, p):
+        @pl.when(self.me.inner)
+        def _():
+            self.copy(0, p).wait_recv()
+            mine, got = self.at(self.part, p), self.at(self.first, p)
+            mine[...] = (mine[...].astype(F32) + got[...].astype(F32)).astype(BF16)
+            self.copy(1, p).start()
+
+    def unfold(self, p):
+        @pl.when(self.me.inner)
+        def _():
+            self.copy(1, p).wait_recv()
+            mine, got, out = self.at(self.part, p), self.at(self.second, p), self.at(self.first, p)
+            out[...] = (mine[...].astype(F32) + got[...].astype(F32)).astype(BF16)
+            self.copy(2, p).start()
+
+    def take(self, p):
+        @pl.when(self.me.outer)
+        def _():
+            self.copy(2, p).wait_recv()
+
+    def drain(self, pieces):
+        def one(p, carry):
+            @pl.when(self.me.outer)
+            def _():
+                self.copy(0, p).wait_send()
+
+            @pl.when(self.me.inner)
+            def _():
+                self.copy(1, p).wait_send()
+                self.copy(2, p).wait_send()
+
+            return carry
+
+        lax.fori_loop(0, pieces, one, 0)
+
+
+class BlockSum:
+    def __init__(self, me, make, out, held, mates, chips, sems):
+        self.me, self.make, self.out = me, make, out
+        self.held, self.mates, self.chips, self.sems = held, mates, chips, sems
+
+    def to_mate(self, k):
+        me = self.me
+        return remote(
+            self.held.at[k % 2], self.mates.at[k], self.sems.at[0, k], self.sems.at[1, k], me.mate, me.t
+        )
+
+    def to_chip(self, k):
+        me = self.me
+        return remote(
+            self.mates.at[k], self.chips.at[k], self.sems.at[2, k], self.sems.at[3, k],
+            me.chip_at(k) * 2 + me.core, me.t,
+        )
+
+    def lend(self, k):
+        me = self.me
+        if k >= 2:
+            self.to_mate(k - 2).wait_send()
+        for lo, hi, value in self.make(me.chip_at(k) * 2 + 1 - me.core):
+            self.held[k % 2, :, lo:hi] = value.astype(BF16)
+        self.to_mate(k).start()
+
+    def step(self, k):
+        me = self.me
+        if k == 0:
+            self.lend(0)
+        if k < 3:
+            self.lend(k + 1)
+        own = self.make(me.chip_at(k) * 2 + me.core)
+        first = True
+        for lo, hi, value in own:
+            if first:
+                self.to_mate(k).wait_recv()
+                first = False
+            total = value + self.mates[k, :, lo:hi].astype(F32)
+            if k < 3:
+                self.mates[k, :, lo:hi] = total.astype(BF16)
+            else:
+                self.out[:, lo:hi] = total
+        if k < 3:
+            self.to_chip(k).start()
+
+    def finish(self):
+        for k in range(3):
+            self.to_chip(k).wait_recv()
+            self.out[...] += self.chips[k].astype(F32)
+        for k in (2, 3):
+            self.to_mate(k).wait_send()
+        for k in range(3):
+            self.to_chip(k).wait_send()
+
+
+def norm_rows(values):
+    inverse = lax.rsqrt(jnp.mean(values * values, axis=-1, keepdims=True) + norm_eps)
+    return values * inverse, inverse
+
+
+def turn(values, cs_ref, sign):
+    cosine, sine = cs_ref[0:HALF, :], cs_ref[HALF:HEAD_SIZE, :] * sign
+    pieces = []
+    for h in range(values.shape[0] // HEAD_SIZE):
+        low = values[h * HEAD_SIZE : h * HEAD_SIZE + HALF]
+        high = values[h * HEAD_SIZE + HALF : (h + 1) * HEAD_SIZE]
+        pieces.append(low * cosine - high * sine)
+        pieces.append(high * cosine + low * sine)
+    return jnp.concatenate(pieces, axis=0)
+
+
+def fill_bias(bias, st_ref, key_start, query_start):
+    key_place = lax.broadcasted_iota(jnp.int32, bias.shape, 0) + key_start
+    query_place = lax.broadcasted_iota(jnp.int32, bias.shape, 1) + query_start
+    allowed = jnp.logical_and(key_place >= st_ref[0:1, :], key_place <= query_place)
+    bias[...] = jnp.where(allowed, 0.0, neg_fill)
+
+
+def heads_of(h, group):
+    g = h // group
+    return slice(h * HEAD_SIZE, (h + 1) * HEAD_SIZE), slice(g * HEAD_SIZE, (g + 1) * HEAD_SIZE), g
+
+
+def forward_kernel(
+    dims,
+    hid_ref, og_ref, st_ref, cs_ref, ag_ref, mg_ref, wq_ref, wk_ref, wv_ref, wo_ref,
+    wg_hbm, wu_hbm, wd_hbm,
+    q_ref, kv_out, ot_ref, lse_ref, br_out, dl_out, mlp_out, act_out, gg_ref, gu_ref,
+    wg, wu, wd, kv, norm, norm_t, og_t, m_ref, l_ref, bias, dh, act, dg, du, mlp,
+    p1, a1, b1, p2, a2, b2, held, mates, chips, total,
+    load_sem, kv_ssem, kv_rsem, sem1, sem2, rs_sem, out_sem,
+):
+    rows, piece, chunk = dims["rows"], dims["piece"], dims["chunk"]
+    q_heads, group, kv_width = dims["q_heads"], dims["group"], dims["kv_width"]
+    n_pieces, n_chunks = rows // piece, rows // chunk
+    per = chunk // piece
+    hidden_units = wg.shape[1]
+    width = hid_ref.shape[1]
+    me = Place()
+    loads = [
+        pltpu.make_async_copy(src, dst, load_sem.at[i])
+        for i, (src, dst) in enumerate(((wd_hbm, wd), (wg_hbm, wg), (wu_hbm, wu)))
+    ]
+    for load in loads:
+        load.start()
+
+    def first_norm(c, carry):
+        r = pl.ds(pl.multiple_of(c * chunk, chunk), chunk)
+        normed, _ = norm_rows(hid_ref[r, :].astype(F32))
+        norm[r, :] = (normed * ag_ref[...]).astype(BF16)
+        return carry
+
+    lax.fori_loop(0, n_chunks, first_norm, 0)
+    key_t = dot_nn(norm[...], wk_ref[...]).T
+    kv[me.b, 0:kv_width, :] = turn(key_t, cs_ref, 1.0).astype(BF16)
+    kv[me.b, kv_width : 2 * kv_width, :] = dot_nn(norm[...], wv_ref[...]).T.astype(BF16)
+    enter(me, (1, 2, 4, 6))
+
+    def kv_copy(s, target):
+        return remote(kv.at[s], kv.at[s], kv_ssem, kv_rsem, target, me.t)
+
+    def send_kv(slot, target, n):
+        return remote(kv.at[slot], kv.at[slot], kv_ssem.at[n], kv_rsem.at[n], target, me.t)
+
+    for s in (6, 4, 2, 1):
+        send_kv(me.b, me.slot(s), s).start()
+    q_ref[...] = turn(dot_nn(norm[...], wq_ref[...]).T, cs_ref, 1.0).astype(BF16)
+    og_t[...] = og_ref[...].T
+
+    m_ref[...] = jnp.full(m_ref.shape, neg_fill, F32)
+    l_ref[...] = jnp.zeros(l_ref.shape, F32)
+    ot_ref[...] = jnp.zeros(ot_ref.shape, F32)
+    loads[0].wait()
+    dh[...] = dot_nt(og_ref[...], wd[...])
+
+    def attend(s, carry):
+        slot = me.slot(s)
+
+        @pl.when(s > 0)
+        def _():
+            send_kv(slot, me.mate, s).wait_recv()
+
+        @pl.when(jnp.logical_and(s > 0, s % 2 == 0))
+        def _():
+            send_kv(slot, me.mate, s + 1).start()
+
+        @pl.when(slot <= me.b)
+        def _():
+            fill_bias(bias, st_ref, slot * rows, me.b * rows)
+            for h in range(q_heads):
+                qs, ks, g = heads_of(h, group)
+                vs = slice(kv_width + g * HEAD_SIZE, kv_width + (g + 1) * HEAD_SIZE)
+                scores = dot_tn(kv[slot, ks, :], q_ref[qs, :]) + bias[...]
+                old = m_ref[h : h + 1, :]
+                new = jnp.maximum(old, jnp.max(scores, axis=0, keepdims=True))
+                probs = jnp.exp2((scores - new) * (SCORE_SCALE * LOG2E))
+                keep = jnp.exp2((old - new) * (SCORE_SCALE * LOG2E))
+                m_ref[h : h + 1, :] = new
+                l_ref[h : h + 1, :] = l_ref[h : h + 1, :] * keep + jnp.sum(probs, axis=0, keepdims=True)
+                ot_ref[qs, :] = ot_ref[qs, :] * keep + dot_nn(kv[slot, vs, :], probs.astype(BF16))
+
+        return carry
+
+    lax.fori_loop(0, 8, attend, 0)
+    for h in range(q_heads):
+        qs, _, _ = heads_of(h, group)
+        ot_ref[qs, :] = ot_ref[qs, :] / l_ref[h : h + 1, :]
+    lse_ref[...] = jnp.zeros(lse_ref.shape, F32)
+    lse_ref[0:q_heads, :] = m_ref[0:q_heads, :] * (SCORE_SCALE * LOG2E) + jnp.log2(l_ref[0:q_heads, :])
+    kv_save = pltpu.make_async_copy(kv, kv_out, out_sem.at[0])
+    kv_save.start()
+
+    branch = LineSum(me, p1, a1, b1, sem1, piece)
+    attn_low = ot_ref[...].T.astype(BF16)
+    for n in range(0, width, 512):
+        p1[:, n : n + 512] = dot_nn(attn_low, wo_ref[:, n : n + 512]).astype(BF16)
+
+    def each(f, lo, hi):
+        def one(p, carry):
+            f(p)
+            return carry
+
+        lax.fori_loop(lo, hi, one, 0)
+
+    each(branch.give, 0, n_pieces)
+    each(branch.fold, 0, per)
+    loads[1].wait()
+    loads[2].wait()
+    back = LineSum(me, p2, a2, b2, sem2, piece)
+
+    def feed(c, carry):
+        @pl.when(c < n_chunks - 1)
+        def _():
+            each(branch.fold, (c + 1) * per, (c + 2) * per)
+
+        each(branch.unfold, c * per, (c + 1) * per)
+        each(branch.take, c * per, (c + 1) * per)
+        r = pl.ds(pl.multiple_of(c * chunk, chunk), chunk)
+        middle = hid_ref[r, :].astype(F32) + a1[r, :].astype(F32)
+        normed, _ = norm_rows(middle)
+        norm[r, :] = (normed * mg_ref[...]).astype(BF16)
+        for n in range(0, hidden_units, 512):
+            ns = slice(n, n + 512)
+            gate = dot_nn(norm[r, :], wg[:, ns])
+            up = dot_nn(norm[r, :], wu[:, ns])
+            sig = 1.0 / (1.0 + jnp.exp(-gate))
+            silu = gate * sig
+            act[r, ns] = (silu * up).astype(BF16)
+            grad = dh[r, ns]
+            dg[r, ns] = (grad * up * sig * (1.0 + gate * (1.0 - sig))).astype(BF16)
+            du[r, ns] = (grad * silu).astype(BF16)
+        for n in range(0, width, 512):
+            ns = slice(n, n + 512)
+            p2[r, ns] = (dot_nt(dg[r, :], wg[ns, :]) + dot_nt(du[r, :], wu[ns, :])).astype(BF16)
+        each(back.give, c * per, (c + 1) * per)
+
+        @pl.when(c >= 1)
+        def _():
+            each(back.fold, (c - 1) * per, c * per)
+
+        @pl.when(c >= 2)
+        def _():
+            each(back.unfold, (c - 2) * per, (c - 1) * per)
+
+        return carry
+
+    lax.fori_loop(0, n_chunks, feed, 0)
+    br_save = pltpu.make_async_copy(a1, br_out, out_sem.at[1])
+    br_save.start()
+    act_save = pltpu.make_async_copy(act, act_out, out_sem.at[2])
+    act_save.start()
+    each(back.fold, n_pieces - per, n_pieces)
+    each(back.unfold, n_pieces - 2 * per, n_pieces - per)
+    norm_t[...] = norm[...].T
+
+    def products(j):
+        js = pl.ds(pl.multiple_of(j * dims["share"], dims["share"]), dims["share"])
+        yield 0, hidden_units, dot_nn(norm_t[js, :], dg[...])
+        yield hidden_units, 2 * hidden_units, dot_nn(norm_t[js, :], du[...])
+
+    weight_sum = BlockSum(me, products, total, held, mates, chips, rs_sem)
+    weight_sum.step(0)
+    each(back.unfold, n_pieces - per, n_pieces)
+    for k in range(1, 4):
+        weight_sum.step(k)
+    for n in range(0, width, 512):
+        mlp[:, n : n + 512] = dot_nn(act[...], wd[:, n : n + 512]).astype(BF16)
+    mlp_save = pltpu.make_async_copy(mlp, mlp_out, out_sem.at[3])
+    mlp_save.start()
+    each(back.take, 0, n_pieces)
+    dl_save = pltpu.make_async_copy(a2, dl_out, out_sem.at[4])
+    dl_save.start()
+    weight_sum.finish()
+    gg_ref[...] = total[:, 0:hidden_units]
+    gu_ref[...] = total[:, hidden_units : 2 * hidden_units]
+    for s in (6, 4, 2, 1):
+        send_kv(me.b, me.slot(s), s).wait_send()
+    for s in (2, 4, 6):
+        send_kv(me.slot(s), me.mate, s + 1).wait_send()
+    branch.drain(n_pieces)
+    back.drain(n_pieces)
+    for save in (kv_save, br_save, act_save, mlp_save, dl_save):
+        save.wait()
+
+
+def backward_kernel(
+    dims,
+    hid_ref, og_ref, br_ref, dl_ref, st_ref, cs_ref, ag_ref, mg_ref, q_ref, kv_ref, ot_ref, lse_ref,
+    act_ref, wq_ref, wk_ref, wv_ref, wo_ref, mlp_hbm,
+    lo_ref, ig_ref, gq_ref, gk_ref, gv_ref, go_ref, gd_ref, gains_ref,
+    p3, a3, b3, p4, a4, b4, dmid, dbr, dbr_t, og_t, norm_t, do_t, delta, dq, acc, bias, low_t, dqr, dkr, dvr,
+    kv_held, kv_mates, kv_chips, held1, mates1, chips1, total1, held2, mates2, chips2, total2, gain, gain_in,
+    load_sem, sem3, sem4, kvs_sem, rs1_sem, rs2_sem, gain_ssem, gain_rsem,
+):
+    rows, piece, chunk, share = dims["rows"], dims["piece"], dims["chunk"], dims["share"]
+    q_heads, group, kv_width = dims["q_heads"], dims["group"], dims["kv_width"]
+    n_pieces, n_chunks = rows // piece, rows // chunk
+    per = chunk // piece
+    width = hid_ref.shape[1]
+    hidden_units = act_ref.shape[1]
+    q_width = q_heads * HEAD_SIZE
+    me = Place()
+    load = pltpu.make_async_copy(mlp_hbm, p3, load_sem)
+    load.start()
+    enter(me, tuple(range(1, 8)))
+    load.wait()
+
+    def each(f, lo, hi):
+        def one(p, carry):
+            f(p)
+            return carry
+
+        lax.fori_loop(lo, hi, one, 0)
+
+    branch = LineSum(me, p3, a3, b3, sem3, piece)
+    each(branch.give, 0, n_pieces)
+    gain[...] = jnp.zeros(gain.shape, F32)
+
+    def middle_grad(c, carry):
+        r = pl.ds(pl.multiple_of(c * chunk, chunk), chunk)
+        normed, inverse = norm_rows(hid_ref[r, :].astype(F32) + br_ref[r, :].astype(F32))
+        grad = dl_ref[r, :].astype(F32)
+        scaled = grad * mg_ref[...]
+        gain[1:2, :] += jnp.sum(grad * normed, axis=0, keepdims=True)
+        found = og_ref[r, :].astype(F32) + inverse * (
+            scaled - normed * jnp.mean(scaled * normed, axis=-1, keepdims=True)
+        )
+        dmid[r, :] = found
+        dbr[r, :] = found.astype(BF16)
+        return carry
+
+    lax.fori_loop(0, n_chunks, middle_grad, 0)
+    do_t[...] = dot_nt(wo_ref[...], dbr[...]).astype(BF16)
+    delta[...] = jnp.zeros(delta.shape, F32)
+    for h in range(q_heads):
+        qs, _, _ = heads_of(h, group)
+        delta[h : h + 1, :] = jnp.sum(do_t[qs, :].astype(F32) * ot_ref[qs, :], axis=0, keepdims=True)
+    dq[...] = jnp.zeros(dq.shape, F32)
+
+    def kv_to_mate(k):
+        return remote(kv_held.at[k], kv_mates.at[k], kvs_sem.at[0, k], kvs_sem.at[1, k], me.mate, me.t)
+
+    def kv_to_chip(k):
+        return remote(
+            kv_mates.at[k], kv_chips.at[k], kvs_sem.at[2, k], kvs_sem.at[3, k],
+            me.chip_at(k) * 2 + me.core, me.t,
+        )
+
+    def attend(u, carry):
+        k, own = u // 2, u % 2
+        chip = me.chip_at(k)
+        slot = chip * 2 + (me.core + 1 - own) % 2
+        branch.fold(u)
+
+        @pl.when(u >= 1)
+        def _():
+            branch.unfold(u - 1)
+
+        @pl.when(slot <= me.b)
+        def _():
+            fill_bias(bias, st_ref, slot * rows, me.b * rows)
+            for g in range(q_heads // group):
+                ks = slice(g * HEAD_SIZE, (g + 1) * HEAD_SIZE)
+                vs = slice(kv_width + g * HEAD_SIZE, kv_width + (g + 1) * HEAD_SIZE)
+                key_t, value_t = kv_ref[slot, ks, :], kv_ref[slot, vs, :]
+                grad_k = grad_v = None
+                for h in range(g * group, (g + 1) * group):
+                    qs, _, _ = heads_of(h, group)
+                    query_t, grad_t = q_ref[qs, :], do_t[qs, :]
+                    scores = dot_tn(key_t, query_t) + bias[...]
+                    probs = jnp.exp2(scores * (SCORE_SCALE * LOG2E) - lse_ref[h : h + 1, :])
+                    grad_p = dot_tn(value_t, grad_t)
+                    grad_s = (probs * (grad_p - delta[h : h + 1, :])).astype(BF16)
+                    one_v = dot_nt(grad_t, probs.astype(BF16))
+                    one_k = dot_nt(query_t, grad_s)
+                    grad_v = one_v if grad_v is None else grad_v + one_v
+                    grad_k = one_k if grad_k is None else grad_k + one_k
+                    dq[qs, :] += dot_nn(key_t, grad_s)
+                acc[ks, :] = grad_k
+                acc[vs, :] = grad_v
+
+        @pl.when(jnp.logical_and(own == 0, slot <= me.b))
+        def _():
+            kv_held[k] = acc[...].astype(BF16)
+            kv_to_mate(k).start()
+
+        @pl.when(jnp.logical_and(own == 1, chip < me.chip))
+        def _():
+            kv_to_mate(k).wait_recv()
+            kv_mates[k] = (acc[...] + kv_mates[k].astype(F32)).astype(BF16)
+            kv_to_chip(k).start()
+
+        return carry
+
+    lax.fori_loop(0, 8, attend, 0)
+    branch.unfold(n_pieces - 1)
+
+    low_t[0:q_width, :] = turn(dq[...] * SCORE_SCALE, cs_ref, -1.0).astype(BF16)
+    dqr[...] = low_t[0:q_width, :].T
+
+    dbr_t[...] = dbr[...].T
+    og_t[...] = og_ref[...].T
+    attn_low = ot_ref[...].astype(BF16)
+
+    def products1(j):
+        js = pl.ds(pl.multiple_of(j * share, share), share)
+        yield 0, hidden_units, dot_nn(og_t[js, :], act_ref[...])
+        yield hidden_units, hidden_units + q_width, dot_nt(dbr_t[js, :], attn_low)
+
+    sum1 = BlockSum(me, products1, total1, held1, mates1, chips1, rs1_sem)
+    for k in range(4):
+        sum1.step(k)
+
+    def layer_rows(c, carry):
+        each(branch.take, c * per, (c + 1) * per)
+        r = pl.ds(pl.multiple_of(c * chunk, chunk), chunk)
+        middle = hid_ref[r, :].astype(F32) + br_ref[r, :].astype(F32)
+        lo_ref[r, :] = (middle + a3[r, :].astype(F32)).astype(BF16)
+        normed, _ = norm_rows(hid_ref[r, :].astype(F32))
+        dbr[r, :] = (normed * ag_ref[...]).astype(BF16)
+        return carry
+
+    lax.fori_loop(0, n_chunks, layer_rows, 0)
+    norm_t[...] = dbr[...].T
+
+    @pl.when(me.core == 0)
+    def _():
+        kv_to_mate(3).wait_recv()
+        acc[...] += kv_mates[3].astype(F32)
+
+    for k in range(3):
+
+        @pl.when(me.chip_at(k) > me.chip)
+        def _(k=k):
+            kv_to_chip(k).wait_recv()
+            acc[...] += kv_chips[k].astype(F32)
+
+    low_t[q_width : q_width + kv_width, :] = turn(acc[0:kv_width, :] * SCORE_SCALE, cs_ref, -1.0).astype(BF16)
+    low_t[q_width + kv_width : q_width + 2 * kv_width, :] = acc[kv_width : 2 * kv_width, :].astype(BF16)
+    dkr[...] = low_t[q_width : q_width + kv_width, :].T
+    dvr[...] = low_t[q_width + kv_width : q_width + 2 * kv_width, :].T
+
+    last = LineSum(me, p4, a4, b4, sem4, piece)
+
+    def input_part(c, carry):
+        r = pl.ds(pl.multiple_of(c * chunk, chunk), chunk)
+        for n in range(0, width, 512):
+            ns = slice(n, n + 512)
+            p4[r, ns] = (
+                dot_nt(dqr[r, :], wq_ref[ns, :])
+                + dot_nt(dkr[r, :], wk_ref[ns, :])
+                + dot_nt(dvr[r, :], wv_ref[ns, :])
+            ).astype(BF16)
+        each(last.give, c * per, (c + 1) * per)
+        return carry
+
+    lax.fori_loop(0, n_chunks, input_part, 0)
+
+    def products2(j):
+        js = pl.ds(pl.multiple_of(j * share, share), share)
+        yield 0, q_width + 2 * kv_width, dot_nt(norm_t[js, :], low_t[...])
+
+    sum2 = BlockSum(me, products2, total2, held2, mates2, chips2, rs2_sem)
+    each(last.fold, 0, 2)
+    sum2.step(0)
+    each(last.fold, 2, 3)
+    each(last.unfold, 0, 2)
+    sum2.step(1)
+    each(last.fold, 3, 4)
+    each(last.unfold, 2, 3)
+    sum2.step(2)
+    each(last.fold, 4, 5)
+    each(last.unfold, 3, 4)
+    sum2.step(3)
+
+    def rest(p, carry):
+        last.fold(p)
+        last.unfold(p - 1)
+        return carry
+
+    lax.fori_loop(5, n_pieces, rest, 0)
+    last.unfold(n_pieces - 1)
+    sum1.finish()
+    gd_ref[...] = total1[:, 0:hidden_units].T
+    go_ref[...] = total1[:, hidden_units : hidden_units + q_width].T
+
+    def input_rows(c, carry):
+        each(last.take, c * per, (c + 1) * per)
+        r = pl.ds(pl.multiple_of(c * chunk, chunk), chunk)
+        normed, inverse = norm_rows(hid_ref[r, :].astype(F32))
+        grad = a4[r, :].astype(F32)
+        scaled = grad * ag_ref[...]
+        gain[0:1, :] += jnp.sum(grad * normed, axis=0, keepdims=True)
+        found = inverse * (scaled - normed * jnp.mean(scaled * normed, axis=-1, keepdims=True))
+        ig_ref[r, :] = (dmid[r, :] + found).astype(BF16)
+        return carry
+
+    lax.fori_loop(0, n_chunks, input_rows, 0)
+
+    def gain_copy(s):
+        return remote(gain, gain_in.at[s], gain_ssem.at[s], gain_rsem.at[s], me.slot(s), me.t)
+
+    for s in range(1, 8):
+        gain_copy(s).start()
+    sum2.finish()
+    gq_ref[...] = total2[:, 0:q_width]
+    gk_ref[...] = total2[:, q_width : q_width + kv_width]
+    gv_ref[...] = total2[:, q_width + kv_width : q_width + 2 * kv_width]
+    for s in range(1, 8):
+        gain_copy(s).wait_recv()
+    gains = gain[...]
+    for s in range(1, 8):
+        gains = gains + gain_in[s]
+    gains_ref[...] = gains
+    for s in range(1, 8):
+        gain_copy(s).wait_send()
+    branch.drain(n_pieces)
+    last.drain(n_pieces)
+    for k in range(4):
+        chip = me.chip_at(k)
+        slot = chip * 2 + 1 - me.core
+
+        @pl.when(slot <= me.b)
+        def _(k=k):
+            kv_to_mate(k).wait_send()
+
+        if k < 3:
+
+            @pl.when(chip < me.chip)
+            def _(k=k):
+                kv_to_chip(k).wait_send()
+
+
+def kernel_shards(
+    hidden_in, out_grad, lengths, attn_gain, w_query, key_projection_weight, value_projection_weight,
+    w_out, mlp_gain, w_gate, w_up, w_down,
+):
+    rows, width = hidden_in.shape
+    q_width, kv_width = w_query.shape[1], key_projection_weight.shape[1]
+    hidden_units = w_gate.shape[1]
+    blocks = lax.axis_size("blk")
+    share = width // blocks
+    piece, chunk = rows // 8, rows // 4
+    pieces = rows // piece
+    dims = dict(
+        rows=rows, piece=piece, chunk=chunk, share=share, q_heads=q_width // HEAD_SIZE,
+        group=q_width // kv_width, kv_width=kv_width,
+    )
+    places = lax.axis_index("blk") * rows + jnp.arange(rows, dtype=jnp.int32)
+    start = jnp.zeros((rows,), jnp.int32)
+    end = jnp.int32(0)
+    for k in range(lengths.shape[0]):
+        end = end + lengths[k]
+        start = jnp.where(places >= end, end, start)
+    position = (places - start).astype(F32)
+    freqs = rope_base ** (-(2.0 * jnp.arange(HALF, dtype=F32)) / HEAD_SIZE)
+    angle = freqs[:, None] * position[None, :]
+    turns = jnp.concatenate([jnp.cos(angle), jnp.sin(angle)], axis=0)
+    starts = jnp.broadcast_to(start[None, :], (8, rows))
+    attn_gain, mlp_gain = attn_gain[None, :], mlp_gain[None, :]
+    vmem, hbm = pl.BlockSpec(memory_space=pltpu.VMEM), pl.BlockSpec(memory_space=pl.ANY)
+    dma = pltpu.SemaphoreType.DMA
+
+    def shape(dtype, *dims_):
+        return jax.ShapeDtypeStruct(dims_, dtype)
+
+    def low(*dims_):
+        return pltpu.VMEM(dims_, BF16)
+
+    def full(*dims_):
+        return pltpu.VMEM(dims_, F32)
+
+    line = [low(rows, width)] * 3
+    mlp_width = 2 * hidden_units
+
+    def block_buffers(columns):
+        return [
+            low(2, share, columns), low(4, share, columns), low(3, share, columns), full(share, columns),
+        ]
+
+    outs = pl.pallas_call(
+        functools.partial(forward_kernel, dims),
+        out_shape=(
+            shape(BF16, q_width, rows), shape(BF16, blocks, 2 * kv_width, rows), shape(F32, q_width, rows),
+            shape(F32, 8, rows), shape(BF16, rows, width), shape(BF16, rows, width), shape(BF16, rows, width),
+            shape(BF16, rows, hidden_units), shape(F32, share, hidden_units), shape(F32, share, hidden_units),
+        ),
+        in_specs=[vmem] * 10 + [hbm] * 3,
+        out_specs=(vmem, hbm, vmem, vmem, hbm, hbm, hbm, hbm, vmem, vmem),
+        scratch_shapes=[
+            low(width, hidden_units), low(width, hidden_units), low(hidden_units, width),
+            low(blocks, 2 * kv_width, rows), low(rows, width), low(width, rows), low(width, rows),
+            full(8, rows), full(8, rows), full(rows, rows), full(rows, hidden_units),
+            low(rows, hidden_units), low(rows, hidden_units), low(rows, hidden_units), low(rows, width),
+            *line, *line, *block_buffers(mlp_width),
+            dma((3,)), dma((8,)), dma((8,)), dma((6, pieces)), dma((6, pieces)), dma((4, 4)), dma((5,)),
+        ],
+        compiler_params=pltpu.CompilerParams(
+            collective_id=0, has_side_effects=True, vmem_limit_bytes=VMEM_BYTES
+        ),
+    )(
+        hidden_in, out_grad, starts, turns, attn_gain, mlp_gain, w_query, key_projection_weight,
+        value_projection_weight, w_out, w_gate, w_up, w_down,
+    )
+    query_t, kv, attn_t, log_sum, branch, grad_ln, mlp_part, act, grad_gate, grad_up = outs
+    outs = pl.pallas_call(
+        functools.partial(backward_kernel, dims),
+        out_shape=(
+            shape(BF16, rows, width), shape(BF16, rows, width), shape(F32, share, q_width),
+            shape(F32, share, kv_width), shape(F32, share, kv_width), shape(F32, q_width, share),
+            shape(F32, hidden_units, share), shape(F32, 8, width),
+        ),
+        in_specs=[vmem] * 17 + [hbm],
+        out_specs=(vmem,) * 8,
+        scratch_shapes=[
+            *line, *line, full(rows, width), low(rows, width), low(width, rows), low(width, rows),
+            low(width, rows), low(q_width, rows), full(8, rows), full(q_width, rows), full(2 * kv_width, rows),
+            full(rows, rows), low(q_width + 2 * kv_width, rows), low(rows, q_width), low(rows, kv_width),
+            low(rows, kv_width),
+            low(4, 2 * kv_width, rows), low(4, 2 * kv_width, rows), low(3, 2 * kv_width, rows),
+            *block_buffers(hidden_units + q_width), *block_buffers(q_width + 2 * kv_width),
+            full(8, width), full(8, 8, width),
+            dma(()), dma((6, pieces)), dma((6, pieces)), dma((4, 4)), dma((4, 4)), dma((4, 4)),
+            dma((8,)), dma((8,)),
+        ],
+        compiler_params=pltpu.CompilerParams(
+            collective_id=1, has_side_effects=True, vmem_limit_bytes=VMEM_BYTES
+        ),
+    )(
+        hidden_in, out_grad, branch, grad_ln, starts, turns, attn_gain, mlp_gain, query_t, kv, attn_t, log_sum,
+        act, w_query, key_projection_weight, value_projection_weight, w_out, mlp_part,
+    )
+    layer_out, input_grad, grad_query, grad_key, grad_value, grad_out, grad_down, gains = outs
+    mine = lax.dynamic_slice_in_dim(gains[0:2], lax.axis_index("blk") * share, share, 1)
+    return (
+        layer_out, input_grad, grad_query, grad_key, grad_value, grad_out, grad_gate, grad_up, grad_down,
+        mine[0], mine[1],
+    )
+
+
 def solution(mesh):
+    sizes = dict(mesh.shape)
+    small = sizes["blk"] == 8 and sizes["tp"] == 4
     placed = (
         P("blk", None),
         P("blk", None),
@@ -327,7 +1076,7 @@
         P("tp", None),
     )
     return jax.shard_map(
-        shards,
+        kernel_shards if small else shards,
         mesh=mesh,
         in_specs=placed,
         out_specs=(

time: 1180 us -> 308 us (0.26)
  waiting for transfers between devices: 987 us -> 0 us
  Pallas kernels: 0 us -> 283 us
  matrix products: 77.4 us -> 0 us
  other arithmetic: 38.7 us -> 1.78 us
  blocking collectives: 24.1 us -> 0 us
  between operations: 15.8 us -> 3.98 us
    psum x3 -> x0, waiting for transfers between devices: 491 us -> none  [the longest x1 186 us: shards(): lax.psum(jnp.dot(attn_low, w_out, preferred_element_type=jnp.float32), 'tp')]
    reduce_scatter x8 -> x0, waiting for transfers between devices: 463 us -> none  [the longest x1 125 us: shards(): lax.psum_scatter(grad_kv_all, 'blk', scatter_dimension=0, tiled=True)]
    pallas_call x0 -> x2, Pallas kernels: none -> 283 us  [the longest x1 161 us: kernel_shards(): pl.pallas_call(functools.partial(forward_kernel, dims), out_shape=(shape(...]
    dot_general x28 -> x0, matrix products: 77.4 us -> none  [the longest x7 34.1 us: left_product(): lax.dot_general(left_side, right_side, (((0,), (0,)), ((), ())), preferre...]
    all_gather x1 -> x0, waiting for transfers between devices: 32.8 us -> none  [shards(): piece = lax.all_gather(kv_rows, 'blk', axis=0, tiled=True)]
    unnamed x1 -> x0, blocking collectives: 24.1 us -> none
    reduce_sum x9 -> x0, other arithmetic: 16.4 us -> none  [the longest x2 7.55 us: norm_back(): return (grad_values, jnp.sum(grad_in * normed, axis=0))]
  transfers between devices with their start and end apart: 12 -> 0, of which waited for: 12 -> 0; matrix products, arithmetic and copies ran while one was open for 5% -> 0% of each run, Pallas kernels for 0% -> 0%
where the time goes in v1:
time: 308 us
  Pallas kernels  283 us (92%)
  local copies, waits for them, and re-layouts  19.4 us (6%)
  between operations  3.98 us (1%)
    pallas_call x1, Pallas kernels, kernel_shards(): pl.pallas_call(functools.partial(forward_kernel, dims), out_shape=(shape(...  161 us
    pallas_call x1, Pallas kernels, kernel_shards(): pl.pallas_call(functools.partial(backward_kernel, dims), out_shape=(shape...  122 us
    unnamed x31, local copies, waits for them, and re-layouts  14.8 us

profile of v1, /device:TPU:0, one launch (start us, length us, event | category | flops | bytes accessed | tf_op | source)
XLA Modules:
  0.0 307.9 jit_solution(1317072152660682740)
XLA Ops:
  0.6 0.0 copy-start.4
  0.7 1.4 fusion.1
  5.3 0.7 subtract_convert_fusion
  6.0 0.4 multiply_cosine_fusion
  6.4 0.0 copy-start.8
  6.5 0.0 copy-start.9
  6.5 0.7 pad_maximum_fusion.cs_ref
  7.2 0.6 broadcast_in_dim.24.st_ref
  7.8 2.2 copy.23.wk_ref
  10.0 0.0 copy-done.4
  10.0 1.2 copy.24.wv_ref
  11.1 0.0 copy-done.8
  11.1 0.6 broadcast_in_dim.25.ag_ref
  11.7 0.0 copy-done.9
  11.7 0.6 broadcast_in_dim.26.mg_ref
  12.3 160.5 %shard_map.203 = (bf16[384,512]{1,0:T(8,128)(2,1)}, bf16[8,384,512]{2,1,0:T(8,128)(2,1)}, f32[384,512]{1,0:T(8,128)}, f32[8,512]{1,0:T(8,128)}, bf16[512,1536]{1...) custom-call(bf16[512,1536]{1,0:T(8,128)(2,1)} %hid_ref.3, ...), custom_call_target="tpu_custom_call" | custom-call | tf_op jit(solution)/shard_map/pallas_call | solution.py:1001
  172.9 122.2 %shard_map.204 = (bf16[512,1536]{1,0:T(8,128)(2,1)}, bf16[512,1536]{1,0:T(8,128)(2,1)}, f32[192,384]{1,0:T(8,128)}, f32[192,192]{1,0:T(8,128)}, f32[192,192]{1,0...) custom-call(bf16[512,1536]{1,0:T(8,128)(2,1)} %hid_ref.3, bf16[512,1536]{1,0:T(8,128)(2,1)} %og_ref.3, ...), custom_call_target="tpu_custom_call" | custom-call | tf_op jit(solution)/shard_map/pallas_call | solution.py:1026
  295.1 2.5 copy.28
  297.6 1.9 copy.27
  299.5 0.8 slice.29
  300.3 0.6 fusion
  300.9 1.1 copy.36
  302.1 0.8 copy-done
  302.9 1.1 copy.37
  304.1 0.7 copy.38
  304.8 0.0 copy-done.7
  304.8 0.7 copy.39
  305.5 0.0 copy-done.6
  305.5 0.7 copy.40
  306.1 0.0 copy-done.3
  306.2 0.9 copy.41
  307.0 0.9 copy.42
  (11 shorter events, 0.0 us)
Async XLA Ops:
  0.6 9.3 %copy-start.4 = (bf16[1536,192]{0,1:T(8,128)(2,1)S(1)}, bf16[1536,192]{0,1:T(8,128)(2,1)}, u32[]{:S(2)}) copy-start(bf16[1536,192]{0,1:T(8,128)(2,1)} %param.18) | copy-start | bytes 1769476
  6.4 4.7 %copy-start.8 = (f32[1536]{0:T(1024)S(1)}, f32[1536]{0:T(1024)}, u32[]{:S(2)}) copy-start(f32[1536]{0:T(1024)} %param.15) | copy-start | bytes 18436
  6.5 5.3 %copy-start.9 = (f32[1536]{0:T(1024)S(1)}, f32[1536]{0:T(1024)}, u32[]{:S(2)}) copy-start(f32[1536]{0:T(1024)} %param.20) | copy-start | bytes 18436
  295.1 5.9 %copy-start.1 = (bf16[512,1536]{1,0:T(8,128)(2,1)S(1)}, bf16[512,1536]{1,0:T(8,128)(2,1)}, u32[]{:S(2)}) copy-start(bf16[512,1536]{1,0:T(8,128)(2,1)} %get-tuple-element.80) | copy-start | bytes 4718596
  300.9 2.0 copy-start
  302.9 1.2 copy-start.5
  302.9 1.9 copy-start.7
  302.9 2.6 copy-start.6
  302.9 3.2 %copy-start.3 = (f32[192,1024]{1,0:T(8,128)S(1)}, f32[192,1024]{1,0:T(8,128)}, u32[]{:S(2)}) copy-start(f32[192,1024]{1,0:T(8,128)} %get-tuple-element.86) | copy-start | bytes 2359300
  304.1 3.0 copy-start.2

commit v2 on v0

--- a/solution.py
+++ b/solution.py
@@ -1,6 +1,11 @@
+import functools
+import math
+
 import jax
 import jax.numpy as jnp
 from jax import lax
+from jax.experimental import pallas as pl
+from jax.experimental.pallas import tpu as pltpu
 from jax.sharding import PartitionSpec as P
 
 HEAD_SIZE = 96
@@ -311,7 +316,884 @@
     )
 
 
+MESH = pl.DeviceIdType.MESH
+F32, BF16 = jnp.float32, jnp.bfloat16
+LOG2E = 1.4426950408889634
+SCORE_SCALE = HEAD_SIZE**-0.5
+VMEM_BYTES = 64 * 2**20 - 2**19
+HALF = HEAD_SIZE // 2
+
+
+def dot_nn(a, b):
+    return lax.dot_general(a, b, (((1,), (0,)), ((), ())), preferred_element_type=F32)
+
+
+def dot_nt(a, b):
+    return lax.dot_general(a, b, (((1,), (1,)), ((), ())), preferred_element_type=F32)
+
+
+def dot_tn(a, b):
+    return lax.dot_general(a, b, (((0,), (0,)), ((), ())), preferred_element_type=F32)
+
+
+class Place:
+    def __init__(self):
+        self.b = lax.axis_index("blk")
+        self.t = lax.axis_index("tp")
+        self.core = self.b % 2
+        self.chip = self.b // 2
+        self.x = self.chip % 2
+        self.y = self.b // 4
+        self.mate = self.b + 1 - 2 * self.core
+        self.inner = jnp.logical_or(self.t == 1, self.t == 2)
+        self.outer = jnp.logical_not(self.inner)
+        self.pair = self.t + 1 - 2 * (self.t % 2)
+        self.across = 3 - self.t
+
+    def slot(self, s):
+        core = (self.core + s % 2) % 2
+        x = (self.x + (s // 2) % 2) % 2
+        y = (self.y + s // 4) % 2
+        return (y * 2 + x) * 2 + core
+
+    def chip_at(self, k):
+        x = (self.x + (k + 1) % 2) % 2
+        y = (self.y + 1 - k // 2) % 2
+        return y * 2 + x
+
+
+def remote(src, dst, ssem, rsem, b, t):
+    return pltpu.make_async_remote_copy(
+        src_ref=src, dst_ref=dst, send_sem=ssem, recv_sem=rsem, device_id=(b, t), device_id_type=MESH
+    )
+
+
+def enter(me, blk_steps):
+    barrier = pltpu.get_barrier_semaphore()
+    for s in blk_steps:
+        pl.semaphore_signal(barrier, inc=1, device_id=(me.slot(s), me.t), device_id_type=MESH)
+    for z in (me.pair, me.across):
+        pl.semaphore_signal(barrier, inc=1, device_id=(me.b, z), device_id_type=MESH)
+    pl.semaphore_wait(barrier, len(blk_steps) + 2)
+
+
+class LineSum:
+    def __init__(self, me, part, first, second, sems, rows):
+        self.me, self.part, self.first, self.second, self.sems, self.rows = (
+            me, part, first, second, sems, rows,
+        )
+
+    def at(self, ref, p):
+        return ref.at[pl.ds(pl.multiple_of(p * self.rows, self.rows), self.rows), :]
+
+    def copy(self, stage, p):
+        me = self.me
+        src = (self.part, self.part, self.first)[stage]
+        dst = (self.first, self.second, self.first)[stage]
+        target = (me.pair, me.across, me.pair)[stage]
+        return remote(
+            self.at(src, p), self.at(dst, p),
+            self.sems.at[2 * stage, p], self.sems.at[2 * stage + 1, p], me.b, target,
+        )
+
+    def give(self, p):
+        @pl.when(self.me.outer)
+        def _():
+            self.copy(0, p).start()
+
+    def fold(self, p):
+        @pl.when(self.me.inner)
+        def _():
+            self.copy(0, p).wait_recv()
+            mine, got = self.at(self.part, p), self.at(self.first, p)
+            mine[...] = (mine[...].astype(F32) + got[...].astype(F32)).astype(BF16)
+            self.copy(1, p).start()
+
+    def unfold(self, p):
+        @pl.when(self.me.inner)
+        def _():
+            self.copy(1, p).wait_recv()
+            mine, got, out = self.at(self.part, p), self.at(self.second, p), self.at(self.first, p)
+            out[...] = (mine[...].astype(F32) + got[...].astype(F32)).astype(BF16)
+            self.copy(2, p).start()
+
+    def take(self, p):
+        @pl.when(self.me.outer)
+        def _():
+            self.copy(2, p).wait_recv()
+
+    def drain(self, pieces):
+        def one(p, carry):
+            @pl.when(self.me.outer)
+            def _():
+                self.copy(0, p).wait_send()
+
+            @pl.when(self.me.inner)
+            def _():
+                self.copy(1, p).wait_send()
+                self.copy(2, p).wait_send()
+
+            return carry
+
+        lax.fori_loop(0, pieces, one, 0)
+
+
+class LineGather:
+    def __init__(self, me, view, ssem, rsem, last):
+        self.me, self.view, self.ssem, self.rsem, self.last = me, view, ssem, rsem, last
+
+    def copy(self, way, hop, p):
+        t = self.me.t
+
+        def sent():
+            slot = t - (hop - 1) if way == 0 else t + (hop - 1)
+            ref = self.view(slot, p)
+            target = t + 1 if way == 0 else t - 1
+            return remote(ref, ref, self.ssem.at[way, hop - 1, p], self.rsem.at[way, hop - 1, p], self.me.b, target)
+
+        def got():
+            slot = t - hop if way == 0 else t + hop
+            ref = self.view(slot, p)
+            target = t - 1 if way == 0 else t + 1
+            return remote(ref, ref, self.ssem.at[way, hop - 1, p], self.rsem.at[way, hop - 1, p], self.me.b, target)
+
+        return sent, got
+
+    def sends(self, way, hop):
+        t = self.me.t
+        if way == 0:
+            return jnp.logical_and(t - (hop - 1) >= 0, t + 1 <= self.last)
+        return jnp.logical_and(t + (hop - 1) <= self.last, t >= 1)
+
+    def gets(self, way, hop):
+        t = self.me.t
+        return t - hop >= 0 if way == 0 else t + hop <= self.last
+
+    def send(self, hop, p):
+        for way in (0, 1):
+
+            @pl.when(self.sends(way, hop))
+            def _(way=way):
+                self.copy(way, hop, p)[0]().start()
+
+    def step(self, hop, p, also=None):
+        for way in (0, 1):
+
+            @pl.when(self.gets(way, hop))
+            def _(way=way):
+                self.copy(way, hop, p)[1]().wait_recv()
+                if also is not None:
+                    also(way, hop).start()
+
+        if hop < self.last:
+            self.send(hop + 1, p)
+
+    def drain(self, p):
+        for hop in range(1, self.last + 1):
+            for way in (0, 1):
+
+                @pl.when(self.sends(way, hop))
+                def _(way=way, hop=hop):
+                    self.copy(way, hop, p)[0]().wait_send()
+
+
+class BlockSum:
+    def __init__(self, me, make, outs, held, mates, chips, sems):
+        self.me, self.make, self.outs = me, make, outs
+        self.held, self.mates, self.chips, self.sems = held, mates, chips, sems
+
+    def to_mate(self, k):
+        me = self.me
+        return remote(
+            self.held(k % 2), self.mates(k), self.sems.at[0, k], self.sems.at[1, k], me.mate, me.t
+        )
+
+    def to_chip(self, k):
+        me = self.me
+        return remote(
+            self.mates(k), self.chips(k), self.sems.at[2, k], self.sems.at[3, k],
+            me.chip_at(k) * 2 + me.core, me.t,
+        )
+
+    def lend(self, k):
+        me = self.me
+        if k >= 2:
+            self.to_mate(k - 2).wait_send()
+        held = self.held(k % 2)
+        even = me.core == 0
+        for (lo, hi, value), out in zip(self.make(me.chip_at(k)), self.outs):
+            half = value.shape[0] // 2
+            low, high = value[:half], value[half:]
+            held[:, lo:hi] = jnp.where(even, high, low).astype(BF16)
+            out[...] = jnp.where(even, low, high)
+        self.to_mate(k).start()
+
+    def merge(self, k, spans):
+        self.to_mate(k).wait_recv()
+        mates = self.mates(k)
+        for (lo, hi), out in zip(spans, self.outs):
+            total = out[...] + mates[:, lo:hi].astype(F32)
+            if k < 3:
+                mates[:, lo:hi] = total.astype(BF16)
+            else:
+                out[...] = total
+        if k < 3:
+            self.to_chip(k).start()
+
+    def finish(self, spans):
+        for k in range(3):
+            self.to_chip(k).wait_recv()
+            chips = self.chips(k)
+            for (lo, hi), out in zip(spans, self.outs):
+                out[...] += chips[:, lo:hi].astype(F32)
+
+    def drain(self):
+        for k in (2, 3):
+            self.to_mate(k).wait_send()
+        for k in range(3):
+            self.to_chip(k).wait_send()
+
+
+def norm_rows(values):
+    inverse = lax.rsqrt(jnp.mean(values * values, axis=-1, keepdims=True) + norm_eps)
+    return values * inverse, inverse
+
+
+def turn(values, cs_ref, sign):
+    cosine, sine = cs_ref[0:HALF, :], cs_ref[HALF:HEAD_SIZE, :] * sign
+    pieces = []
+    for h in range(values.shape[0] // HEAD_SIZE):
+        low = values[h * HEAD_SIZE : h * HEAD_SIZE + HALF]
+        high = values[h * HEAD_SIZE + HALF : (h + 1) * HEAD_SIZE]
+        pieces.append(low * cosine - high * sine)
+        pieces.append(high * cosine + low * sine)
+    return jnp.concatenate(pieces, axis=0)
+
+
+def fill_bias(bias, st_ref, key_start, query_start):
+    key_place = lax.broadcasted_iota(jnp.int32, bias.shape, 0) + key_start
+    query_place = lax.broadcasted_iota(jnp.int32, bias.shape, 1) + query_start
+    allowed = jnp.logical_and(key_place >= st_ref[0:1, :], key_place <= query_place)
+    bias[...] = jnp.where(allowed, 0.0, neg_fill)
+
+
+def heads_of(h, group):
+    g = h // group
+    return slice(h * HEAD_SIZE, (h + 1) * HEAD_SIZE), slice(g * HEAD_SIZE, (g + 1) * HEAD_SIZE), g
+
+
+def layer_kernel(
+    dims,
+    len_ref, ag_ref, mg_ref, hid_hbm, og_hbm, wq_hbm, wk_hbm, wv_hbm, wo_hbm, wg_hbm, wu_hbm, wd_hbm,
+    lo_out, ig_out, gq_ref, gk_ref, gv_ref, go_ref, gg_ref, gu_ref, gd_ref, gag_ref, gmg_ref,
+    hid, og, wq, wkv, wo, wg, wu, wd, kv, norm, attn, qt, ot, bias, mid, act, dg, du,
+    p2, a2, b2, p3, a3, b3, dbr, dot_ref, dq, acc, low_t, dqr, dkvr,
+    kv_mates, kv_chips, held_a, held_b, chips_b, held_c, mates_c, chips_c, total_c,
+    turns, starts, m_ref, l_ref, lse, delta, gain, gain_in,
+    load_sem, kv_sem, wo_sem, wo_mate_sem, at_sem, sem2, sem3, sem4, kvs_sem, rs_sem, gain_sem, out_sem,
+    mate_ready, chip_ready,
+):
+    rows, piece, chunk, share = dims["rows"], dims["piece"], dims["chunk"], dims["share"]
+    q_heads, group, kv_width, n_docs = dims["q_heads"], dims["group"], dims["kv_width"], dims["n_docs"]
+    n_pieces, n_chunks = rows // piece, rows // chunk
+    per = chunk // piece
+    width, hidden_units = wg.shape
+    q_width = q_heads * HEAD_SIZE
+    last = wo.shape[0] - 1
+    me = Place()
+    scale2 = SCORE_SCALE * LOG2E
+
+    def each(f, lo, hi):
+        def one(p, carry):
+            f(p)
+            return carry
+
+        lax.fori_loop(lo, hi, one, 0)
+
+    barrier = pltpu.get_barrier_semaphore()
+    for s in range(1, 8):
+        pl.semaphore_signal(barrier, inc=1, device_id=(me.slot(s), me.t), device_id_type=MESH)
+    for z in (me.pair, me.across):
+        pl.semaphore_signal(barrier, inc=1, device_id=(me.b, z), device_id_type=MESH)
+    loads = {}
+    for i, (name, source, target) in enumerate((
+        ("hid", hid_hbm, hid), ("wo", wo_hbm, wo.at[me.t]), ("wk", wk_hbm, wkv.at[0:kv_width]),
+        ("wv", wv_hbm, wkv.at[kv_width : 2 * kv_width]), ("wq", wq_hbm, wq), ("wg", wg_hbm, wg),
+        ("wu", wu_hbm, wu), ("og", og_hbm, og), ("wd", wd_hbm, wd),
+    )):
+        loads[name] = pltpu.make_async_copy(source, target, load_sem.at[i])
+        loads[name].start()
+
+    places = me.b * rows + lax.broadcasted_iota(jnp.int32, (1, rows), 1)
+    start, end = jnp.zeros((1, rows), jnp.int32), jnp.int32(0)
+    for k in range(n_docs):
+        end = end + len_ref[k]
+        start = jnp.where(places >= end, end, start)
+    starts[...] = jnp.broadcast_to(start, starts.shape)
+    order = lax.broadcasted_iota(jnp.int32, (HALF, 1), 0).astype(F32)
+    freqs = jnp.exp(order * (-2.0 / HEAD_SIZE * math.log(rope_base)))
+    angle = freqs * (places - start).astype(F32)
+    turns[0:HALF, :] = jnp.cos(angle)
+    turns[HALF:HEAD_SIZE, :] = jnp.sin(angle)
+    attn_gain, mlp_gain = ag_ref[...].reshape(1, width), mg_ref[...].reshape(1, width)
+
+    def chunk_rows(c):
+        return pl.ds(pl.multiple_of(c * chunk, chunk), chunk)
+
+    def first_norm(c):
+        r = chunk_rows(c)
+        normed, _ = norm_rows(hid[r, :].astype(F32))
+        norm[r, :] = (normed * attn_gain).astype(BF16)
+
+    loads["hid"].wait()
+    each(first_norm, 0, n_chunks)
+    loads["wo"].wait()
+    pl.semaphore_wait(barrier, 9)
+
+    my_half = pl.ds(pl.multiple_of(me.core * share, share), share)
+    whole_wo = LineGather(me, lambda slot, p: wo.at[slot, my_half, :], wo_sem.at[0], wo_sem.at[1], last)
+
+    def wo_to_mate(way, hop):
+        slot = me.t - hop if way == 0 else me.t + hop
+        ref = wo.at[slot, my_half, :]
+        return remote(
+            ref, ref, wo_mate_sem.at[0, way, hop - 1], wo_mate_sem.at[1, way, hop - 1], me.mate, me.t
+        )
+
+    whole_wo.send(1, 0)
+
+    loads["wk"].wait()
+    loads["wv"].wait()
+    both_t = dot_nt(wkv[...], norm[...])
+    kv[me.b, 0:kv_width, :] = turn(both_t[0:kv_width], turns, 1.0).astype(BF16)
+    kv[me.b, kv_width : 2 * kv_width, :] = both_t[kv_width : 2 * kv_width].astype(BF16)
+
+    def kv_copy(slot, target, n):
+        return remote(kv.at[slot], kv.at[slot], kv_sem.at[0, n], kv_sem.at[1, n], target, me.t)
+
+    def share_kv(s):
+        @pl.when(me.slot(s) > me.b)
+        def _():
+            kv_copy(me.b, me.slot(s), s).start()
+
+    for s in (1, 2, 4):
+        share_kv(s)
+    loads["wq"].wait()
+    qt[...] = turn(dot_nn(norm[...], wq[...]).T, turns, 1.0).astype(BF16)
+    m_ref[...] = jnp.full(m_ref.shape, neg_fill, F32)
+    l_ref[...] = jnp.zeros(l_ref.shape, F32)
+    ot[...] = jnp.zeros(ot.shape, F32)
+
+    def attend(s, carry):
+        slot = me.slot(s)
+        arrives = jnp.logical_and(s > 0, slot < me.b)
+
+        @pl.when(arrives)
+        def _():
+            kv_copy(slot, me.mate, s).wait_recv()
+
+        @pl.when(jnp.logical_and(arrives, s % 2 == 0))
+        def _():
+            kv_copy(slot, me.mate, s + 1).start()
+
+        @pl.when(s == 5)
+        def _():
+            whole_wo.step(1, 0, wo_to_mate)
+
+        @pl.when(slot <= me.b)
+        def _():
+            fill_bias(bias, starts, slot * rows, me.b * rows)
+            for h in range(q_heads):
+                qs, ks, g = heads_of(h, group)
+                vs = slice(kv_width + g * HEAD_SIZE, kv_width + (g + 1) * HEAD_SIZE)
+                scores = dot_tn(kv[slot, ks, :], qt[qs, :]) + bias[...]
+                old = m_ref[h : h + 1, :]
+                new = jnp.maximum(old, jnp.max(scores, axis=0, keepdims=True))
+                probs = jnp.exp2((scores - new) * scale2)
+                keep = jnp.exp2((old - new) * scale2)
+                m_ref[h : h + 1, :] = new
+                l_ref[h : h + 1, :] = l_ref[h : h + 1, :] * keep + jnp.sum(probs, axis=0, keepdims=True)
+                ot[qs, :] = ot[qs, :] * keep + dot_nn(kv[slot, vs, :], probs.astype(BF16))
+
+        @pl.when(s == 1)
+        def _():
+            share_kv(6)
+
+        return carry
+
+    lax.fori_loop(0, 8, attend, 0)
+    whole_wo.step(2, 0, wo_to_mate)
+
+    line_attn = LineGather(
+        me, lambda slot, p: attn.at[slot, chunk_rows(p), :], at_sem.at[0], at_sem.at[1], last
+    )
+    for h in range(q_heads):
+        qs, _, _ = heads_of(h, group)
+        ot[qs, :] = ot[qs, :] / l_ref[h : h + 1, :]
+    for c in range(n_chunks):
+        attn[me.t, c * chunk : (c + 1) * chunk, :] = ot[:, c * chunk : (c + 1) * chunk].T.astype(BF16)
+        if c < 2:
+            line_attn.send(1, c)
+    lse[...] = jnp.zeros(lse.shape, F32)
+    lse[0:q_heads, :] = m_ref[0:q_heads, :] * scale2 + jnp.log2(l_ref[0:q_heads, :])
+    for name in ("wg", "wu", "og", "wd"):
+        loads[name].wait()
+    for hop in range(1, last + 1):
+        line_attn.step(hop, 0)
+    whole_wo.step(3, 0, wo_to_mate)
+    for hop in range(1, last + 1):
+        for way in (0, 1):
+
+            @pl.when(whole_wo.gets(way, hop))
+            def _(way=way, hop=hop):
+                wo_to_mate(way, hop).wait_recv()
+
+    back = LineSum(me, p2, a2, b2, sem2, piece)
+    forth = LineSum(me, p3, a3, b3, sem3, piece)
+    adds_middle = (me.t == 1).astype(F32)
+
+    def feed(c, carry):
+        r = chunk_rows(c)
+        for n in range(0, width, 512):
+            ns = slice(n, n + 512)
+            total = hid[r, ns].astype(F32)
+            for z in range(last + 1):
+                total = total + dot_nn(attn[z, r, :], wo[z, :, ns])
+            mid[r, ns] = total
+        normed, _ = norm_rows(mid[r, :])
+        norm[r, :] = (normed * mlp_gain).astype(BF16)
+
+        @pl.when(c >= 1)
+        def _():
+            each(back.fold, (c - 1) * per, c * per)
+
+        @pl.when(c < n_chunks - 1)
+        def _():
+            line_attn.step(1, c + 1)
+
+        for n in range(0, hidden_units, 512):
+            ns = slice(n, n + 512)
+            gate = dot_nn(norm[r, :], wg[:, ns])
+            up = dot_nn(norm[r, :], wu[:, ns])
+            grad = dot_nt(og[r, :], wd[ns, :])
+            sig = 1.0 / (1.0 + jnp.exp(-gate))
+            silu = gate * sig
+            act[r, ns] = (silu * up).astype(BF16)
+            dg[r, ns] = (grad * up * sig * (1.0 + gate * (1.0 - sig))).astype(BF16)
+            du[r, ns] = (grad * silu).astype(BF16)
+            if n == 0:
+
+                @pl.when(c < n_chunks - 1)
+                def _():
+                    line_attn.step(2, c + 1)
+
+                @pl.when(c < n_chunks - 2)
+                def _():
+                    line_attn.send(1, c + 2)
+
+        for n in range(0, width, 512):
+            ns = slice(n, n + 512)
+            p2[r, ns] = (dot_nt(dg[r, :], wg[ns, :]) + dot_nt(du[r, :], wu[ns, :])).astype(BF16)
+        each(back.give, c * per, (c + 1) * per)
+
+        @pl.when(c >= 1)
+        def _():
+            each(back.unfold, (c - 1) * per, c * per)
+
+        @pl.when(c < n_chunks - 1)
+        def _():
+            line_attn.step(3, c + 1)
+
+        for n in range(0, width, 512):
+            ns = slice(n, n + 512)
+            p3[r, ns] = (dot_nn(act[r, :], wd[:, ns]) + mid[r, ns] * adds_middle).astype(BF16)
+        return carry
+
+    lax.fori_loop(0, n_chunks, feed, 0)
+    pl.semaphore_signal(mate_ready, inc=1, device_id=(me.mate, me.t), device_id_type=MESH)
+    for k in range(3):
+        pl.semaphore_signal(
+            chip_ready, inc=1, device_id=(me.chip_at(k) * 2 + me.core, me.t), device_id_type=MESH
+        )
+    each(forth.give, 0, n_pieces)
+    pair = 2 * share
+
+    def pair_columns(ref, chip):
+        return ref[:, pl.ds(pl.multiple_of(chip * pair, pair), pair)]
+
+    def slots(ref, first, columns):
+        return lambda k: ref.at[(first + k) * share : (first + k + 1) * share, 0:columns]
+
+    sum_gate = BlockSum(
+        me, lambda m: [(0, hidden_units, dot_tn(pair_columns(norm, m), dg[...]))], [gg_ref],
+        lambda k: held_a.at[0, k], slots(wg, 0, hidden_units), slots(wg, 4, hidden_units), rs_sem.at[0],
+    )
+    sum_up = BlockSum(
+        me, lambda m: [(0, hidden_units, dot_tn(pair_columns(norm, m), du[...]))], [gu_ref],
+        lambda k: held_a.at[1, k], slots(wu, 0, hidden_units), slots(wu, 4, hidden_units), rs_sem.at[1],
+    )
+    span_a = [(0, hidden_units)]
+    pl.semaphore_wait(mate_ready, 1)
+    gain[...] = jnp.zeros(gain.shape, F32)
+
+    def middle_grad(c):
+        each(back.take, c * per, (c + 1) * per)
+        r = chunk_rows(c)
+        normed, inverse = norm_rows(mid[r, :])
+        grad = a2[r, :].astype(F32)
+        scaled = grad * mlp_gain
+        gain[1:2, :] += jnp.sum(grad * normed, axis=0, keepdims=True)
+        found = og[r, :].astype(F32) + inverse * (
+            scaled - normed * jnp.mean(scaled * normed, axis=-1, keepdims=True)
+        )
+        mid[r, :] = found
+        dbr[r, :] = found.astype(BF16)
+
+    sum_gate.lend(0)
+    sum_up.lend(0)
+    each(back.fold, n_pieces - per, n_pieces)
+    pl.semaphore_wait(chip_ready, 3)
+    sum_gate.merge(0, span_a)
+    sum_up.merge(0, span_a)
+    sum_gate.lend(1)
+    sum_up.lend(1)
+    each(back.unfold, n_pieces - per, n_pieces)
+    sum_gate.merge(1, span_a)
+    sum_up.merge(1, span_a)
+    each(middle_grad, 0, n_chunks - 1)
+    sum_gate.lend(2)
+    sum_up.lend(2)
+    each(middle_grad, n_chunks - 1, n_chunks)
+    dot_ref[...] = dot_nt(wo[me.t], dbr[...]).astype(BF16)
+    sum_gate.merge(2, span_a)
+    sum_up.merge(2, span_a)
+    delta[...] = jnp.zeros(delta.shape, F32)
+    for h in range(q_heads):
+        qs, _, _ = heads_of(h, group)
+        delta[h : h + 1, :] = jnp.sum(dot_ref[qs, :].astype(F32) * ot[qs, :], axis=0, keepdims=True)
+    dq[...] = jnp.zeros(dq.shape, F32)
+    back.drain(n_pieces)
+
+    for s in (1, 2, 4, 6):
+
+        @pl.when(me.slot(s) > me.b)
+        def _(s=s):
+            kv_copy(me.b, me.slot(s), s).wait_send()
+
+    for s in (2, 4, 6):
+
+        @pl.when(me.slot(s) < me.b)
+        def _(s=s):
+            kv_copy(me.slot(s), me.mate, s + 1).wait_send()
+
+    def kv_to_mate(k):
+        return remote(
+            kv.at[me.chip_at(k) * 2 + 1 - me.core], kv_mates.at[k], kvs_sem.at[0, k], kvs_sem.at[1, k],
+            me.mate, me.t,
+        )
+
+    def kv_to_chip(k):
+        return remote(
+            kv_mates.at[k], kv_chips.at[k], kvs_sem.at[2, k], kvs_sem.at[3, k],
+            me.chip_at(k) * 2 + me.core, me.t,
+        )
+
+    def attend_back(u, carry):
+        k, own = u // 2, u % 2
+        chip = me.chip_at(k)
+        slot = chip * 2 + (me.core + 1 - own) % 2
+        forth.fold(u)
+
+        @pl.when(u >= 1)
+        def _():
+            forth.unfold(u - 1)
+
+        @pl.when(slot <= me.b)
+        def _():
+            fill_bias(bias, starts, slot * rows, me.b * rows)
+            for g in range(q_heads // group):
+                ks = slice(g * HEAD_SIZE, (g + 1) * HEAD_SIZE)
+                vs = slice(kv_width + g * HEAD_SIZE, kv_width + (g + 1) * HEAD_SIZE)
+                key_t, value_t = kv[slot, ks, :], kv[slot, vs, :]
+                grad_k = grad_v = None
+                for h in range(g * group, (g + 1) * group):
+                    qs, _, _ = heads_of(h, group)
+                    query_t, grad_t = qt[qs, :], dot_ref[qs, :]
+                    scores = dot_tn(key_t, query_t) + bias[...]
+                    probs = jnp.exp2(scores * scale2 - lse[h : h + 1, :])
+                    grad_p = dot_tn(value_t, grad_t)
+                    grad_s = (probs * (grad_p - delta[h : h + 1, :])).astype(BF16)
+                    one_v = dot_nt(grad_t, probs.astype(BF16))
+                    one_k = dot_nt(query_t, grad_s)
+                    grad_v = one_v if grad_v is None else grad_v + one_v
+                    grad_k = one_k if grad_k is None else grad_k + one_k
+                    dq[qs, :] += dot_nn(key_t, grad_s)
+                acc[ks, :] = grad_k
+                acc[vs, :] = grad_v
+
+        @pl.when(jnp.logical_and(own == 0, slot <= me.b))
+        def _():
+            kv[slot] = acc[...].astype(BF16)
+            kv_to_mate(k).start()
+
+        @pl.when(jnp.logical_and(own == 1, chip < me.chip))
+        def _():
+            kv_to_mate(k).wait_recv()
+            kv_mates[k] = (acc[...] + kv_mates[k].astype(F32)).astype(BF16)
+            kv_to_chip(k).start()
+
+        return carry
+
+    lax.fori_loop(0, 8, attend_back, 0)
+    forth.unfold(n_pieces - 1)
+    low_t[0:q_width, :] = turn(dq[...] * SCORE_SCALE, turns, -1.0).astype(BF16)
+    dqr[...] = low_t[0:q_width, :].T
+
+    def first_norm_again(c):
+        r = chunk_rows(c)
+        normed, _ = norm_rows(hid[r, :].astype(F32))
+        norm[r, :] = (normed * attn_gain).astype(BF16)
+
+    sum_gate.lend(3)
+    sum_up.lend(3)
+    each(first_norm_again, 0, n_chunks)
+    sum_gate.merge(3, span_a)
+    sum_up.merge(3, span_a)
+
+    @pl.when(me.core == 0)
+    def _():
+        kv_to_mate(3).wait_recv()
+        acc[...] += kv_mates[3].astype(F32)
+
+    for k in range(3):
+
+        @pl.when(me.chip_at(k) > me.chip)
+        def _(k=k):
+            kv_to_chip(k).wait_recv()
+            acc[...] += kv_chips[k].astype(F32)
+
+    low_t[q_width : q_width + kv_width, :] = turn(acc[0:kv_width, :] * SCORE_SCALE, turns, -1.0).astype(BF16)
+    low_t[q_width + kv_width :, :] = acc[kv_width : 2 * kv_width, :].astype(BF16)
+    dkvr[...] = low_t[q_width:, :].T
+
+    each(forth.take, 0, n_pieces)
+    lo_save = pltpu.make_async_copy(a3, lo_out, out_sem.at[0])
+    lo_save.start()
+    end_sum = LineSum(me, p2, a2, b2, sem4, piece)
+
+    def input_part(c):
+        r = chunk_rows(c)
+        for n in range(0, width, 512):
+            ns = slice(n, n + 512)
+            p2[r, ns] = (dot_nt(dqr[r, :], wq[ns, :]) + dot_nn(dkvr[r, :], wkv[:, ns])).astype(BF16)
+        each(end_sum.give, c * per, (c + 1) * per)
+
+    each(input_part, 0, n_chunks)
+
+    def make_b(m):
+        yield 0, hidden_units, dot_tn(pair_columns(og, m), act[...])
+        yield hidden_units, hidden_units + q_width, dot_tn(pair_columns(dbr, m), attn[me.t])
+
+    def make_c(m):
+        columns = pair_columns(norm, m)
+        yield 0, q_width, dot_tn(columns, dqr[...])
+        yield q_width, q_width + 2 * kv_width, dot_tn(columns, dkvr[...])
+
+    width_b = hidden_units + q_width
+    in_wd = slots(wd, 0, width_b)
+    sum_b = BlockSum(
+        me, make_b, [gd_ref, go_ref], lambda k: held_b.at[k], in_wd,
+        lambda k: in_wd(4) if k == 0 else chips_b.at[k - 1], rs_sem.at[2],
+    )
+    span_b = [(0, hidden_units), (hidden_units, width_b)]
+    total_parts = [total_c.at[:, 0:q_width], total_c.at[:, q_width : q_width + 2 * kv_width]]
+    sum_c = BlockSum(
+        me, make_c, total_parts, lambda k: held_c.at[k], lambda k: mates_c.at[k], lambda k: chips_c.at[k],
+        rs_sem.at[3],
+    )
+    span_c = [(0, q_width), (q_width, q_width + 2 * kv_width)]
+    work = []
+    for sums, spans in ((sum_b, span_b), (sum_c, span_c)):
+        for k in range(4):
+            work.append((sums, k, spans))
+    for p in range(n_pieces):
+        if p >= 1:
+            sums, k, spans = work[p - 1]
+            sums.merge(k, spans)
+        sums, k, spans = work[p]
+        sums.lend(k)
+        end_sum.fold(p)
+        if p >= 1:
+            end_sum.unfold(p - 1)
+    end_sum.unfold(n_pieces - 1)
+    sums, k, spans = work[n_pieces - 1]
+    sums.merge(k, spans)
+
+    def input_rows(c):
+        each(end_sum.take, c * per, (c + 1) * per)
+        r = chunk_rows(c)
+        normed, inverse = norm_rows(hid[r, :].astype(F32))
+        grad = a2[r, :].astype(F32)
+        scaled = grad * attn_gain
+        gain[0:1, :] += jnp.sum(grad * normed, axis=0, keepdims=True)
+        found = inverse * (scaled - normed * jnp.mean(scaled * normed, axis=-1, keepdims=True))
+        dbr[r, :] = (mid[r, :] + found).astype(BF16)
+
+    each(input_rows, 0, n_chunks)
+
+    def gain_copy(s):
+        return remote(gain, gain_in.at[s], gain_sem.at[0, s], gain_sem.at[1, s], me.slot(s), me.t)
+
+    for s in range(1, 8):
+        gain_copy(s).start()
+    ig_save = pltpu.make_async_copy(dbr, ig_out, out_sem.at[1])
+    ig_save.start()
+    sum_gate.finish(span_a)
+    sum_up.finish(span_a)
+    sum_b.finish(span_b)
+    sum_c.finish(span_c)
+    gq_ref[...] = total_c[:, 0:q_width]
+    gk_ref[...] = total_c[:, q_width : q_width + kv_width]
+    gv_ref[...] = total_c[:, q_width + kv_width : q_width + 2 * kv_width]
+    for s in range(1, 8):
+        gain_copy(s).wait_recv()
+    gains = gain[...]
+    for s in range(1, 8):
+        gains = gains + gain_in[s]
+    gain_in[0] = gains
+    mine = jnp.zeros((8, share), F32)
+    for j in range(8):
+        mine = mine + jnp.where(me.b == j, gain_in[0, :, j * share : (j + 1) * share], 0.0)
+    gag_ref[...] = mine[0, :]
+    gmg_ref[...] = mine[1, :]
+
+    for s in range(1, 8):
+        gain_copy(s).wait_send()
+    whole_wo.drain(0)
+    for hop in range(1, last + 1):
+        for way in (0, 1):
+
+            @pl.when(whole_wo.gets(way, hop))
+            def _(way=way, hop=hop):
+                wo_to_mate(way, hop).wait_send()
+
+    each(line_attn.drain, 0, n_chunks)
+    forth.drain(n_pieces)
+    end_sum.drain(n_pieces)
+    for sums in (sum_gate, sum_up, sum_b, sum_c):
+        sums.drain()
+    for k in range(4):
+        chip = me.chip_at(k)
+        slot = chip * 2 + 1 - me.core
+
+        @pl.when(slot <= me.b)
+        def _(k=k):
+            kv_to_mate(k).wait_send()
+
+        if k < 3:
+
+            @pl.when(chip < me.chip)
+            def _(k=k):
+                kv_to_chip(k).wait_send()
+
+    lo_save.wait()
+    ig_save.wait()
+
+
+def hand_over(n, *refs):
+    sources, targets, held, sems = refs[:n], refs[n : 2 * n], refs[2 * n : 3 * n], refs[3 * n]
+    ins = [pltpu.make_async_copy(a, h, sems.at[0, i]) for i, (a, h) in enumerate(zip(sources, held))]
+    outs = [pltpu.make_async_copy(h, b, sems.at[1, i]) for i, (h, b) in enumerate(zip(held, targets))]
+    for copy in ins:
+        copy.start()
+    for first, second in zip(ins, outs):
+        first.wait()
+        second.start()
+    for copy in outs:
+        copy.wait()
+
+
+def kernel_shards(
+    hidden_in, out_grad, lengths, attn_gain, w_query, key_projection_weight, value_projection_weight,
+    w_out, mlp_gain, w_gate, w_up, w_down,
+):
+    rows, width = hidden_in.shape
+    q_width, kv_width = w_query.shape[1], key_projection_weight.shape[1]
+    hidden_units = w_gate.shape[1]
+    blocks, line_size = lax.axis_size("blk"), lax.axis_size("tp")
+    share = width // blocks
+    piece, chunk = rows // 8, rows // 4
+    pieces, chunks = rows // piece, rows // chunk
+    dims = dict(
+        rows=rows, piece=piece, chunk=chunk, share=share, q_heads=q_width // HEAD_SIZE,
+        group=q_width // kv_width, kv_width=kv_width, n_docs=lengths.shape[0],
+    )
+    vmem, hbm = pl.BlockSpec(memory_space=pltpu.VMEM), pl.BlockSpec(memory_space=pl.ANY)
+    smem = pl.BlockSpec(memory_space=pltpu.SMEM)
+    dma, regular = pltpu.SemaphoreType.DMA, pltpu.SemaphoreType.REGULAR
+
+    def shape(dtype, *dims_):
+        return jax.ShapeDtypeStruct(dims_, dtype)
+
+    def low(*dims_):
+        return pltpu.VMEM(dims_, BF16)
+
+    def full(*dims_):
+        return pltpu.VMEM(dims_, F32)
+
+    line = [low(rows, width)] * 3
+    width_b, width_c = hidden_units + q_width, q_width + 2 * kv_width
+    shapes = (
+        shape(BF16, rows, width), shape(BF16, rows, width), shape(F32, share, q_width),
+        shape(F32, share, kv_width), shape(F32, share, kv_width), shape(F32, share, q_width),
+        shape(F32, share, hidden_units), shape(F32, share, hidden_units), shape(F32, share, hidden_units),
+        shape(F32, share), shape(F32, share),
+    )
+    outs = pl.pallas_call(
+        functools.partial(layer_kernel, dims),
+        out_shape=shapes,
+        in_specs=[smem, vmem, vmem] + [hbm] * 9,
+        out_specs=(hbm, hbm) + (vmem,) * 9,
+        scratch_shapes=[
+            low(rows, width), low(rows, width), low(width, q_width), low(2 * kv_width, width),
+            low(line_size, q_width, width), low(width, hidden_units), low(width, hidden_units),
+            low(hidden_units, width), low(blocks, 2 * kv_width, rows), low(rows, width),
+            low(line_size, rows, q_width), low(q_width, rows), full(q_width, rows), full(rows, rows),
+            full(rows, width), low(rows, hidden_units), low(rows, hidden_units), low(rows, hidden_units),
+            *line, *line, low(rows, width), low(q_width, rows), full(q_width, rows), full(2 * kv_width, rows),
+            low(width_c, rows), low(rows, q_width), low(rows, 2 * kv_width),
+            low(4, 2 * kv_width, rows), low(3, 2 * kv_width, rows),
+            low(2, 2, share, hidden_units), low(2, share, width_b), low(2, share, width_b),
+            low(2, share, width_c), low(4, share, width_c), low(3, share, width_c), full(share, width_c),
+            full(HEAD_SIZE, rows), pltpu.VMEM((8, rows), jnp.int32), full(8, rows), full(8, rows), full(8, rows),
+            full(8, rows), full(8, width), full(8, 8, width),
+            dma((9,)), dma((2, 8)), dma((2, 2, line_size - 1, 1)), dma((2, 2, line_size - 1)),
+            dma((2, 2, line_size - 1, chunks)), dma((6, pieces)), dma((6, pieces)), dma((6, pieces)),
+            dma((4, 4)), dma((4, 4, 4)), dma((2, 8)), dma((2,)), regular, regular,
+        ],
+        compiler_params=pltpu.CompilerParams(
+            collective_id=0, has_side_effects=True, vmem_limit_bytes=VMEM_BYTES
+        ),
+    )(
+        lengths, attn_gain, mlp_gain, hidden_in, out_grad, w_query, key_projection_weight.T,
+        value_projection_weight.T, w_out, w_gate, w_up, w_down,
+    )
+    outs = pl.pallas_call(
+        functools.partial(hand_over, len(shapes)),
+        out_shape=shapes,
+        in_specs=[hbm] * len(shapes),
+        out_specs=(hbm,) * len(shapes),
+        scratch_shapes=[pltpu.VMEM(s.shape, s.dtype) for s in shapes] + [dma((2, len(shapes)))],
+    )(*outs)
+    layer_out, input_grad, grad_query, grad_key, grad_value, grad_out, grad_gate, grad_up, grad_down, g1, g2 = outs
+    return (
+        layer_out, input_grad, grad_query, grad_key, grad_value, grad_out.T, grad_gate, grad_up, grad_down.T, g1, g2,
+    )
+
+
 def solution(mesh):
+    sizes = dict(mesh.shape)
+    small = sizes["blk"] == 8 and sizes["tp"] == 4
     placed = (
         P("blk", None),
         P("blk", None),
@@ -327,7 +1209,7 @@
         P("tp", None),
     )
     return jax.shard_map(
-        shards,
+        kernel_shards if small else shards,
         mesh=mesh,
         in_specs=placed,
         out_specs=(

time: 1180 us -> 248 us (0.21)
  waiting for transfers between devices: 987 us -> 0 us
  Pallas kernels: 0 us -> 246 us
  matrix products: 77.4 us -> 0 us
  other arithmetic: 38.7 us -> 0 us
  blocking collectives: 24.1 us -> 0 us
  local copies, waits for them, and re-layouts: 24 us -> 0 us
  between operations: 15.8 us -> 0.84 us
    psum x3 -> x0, waiting for transfers between devices: 491 us -> none  [the longest x1 186 us: shards(): lax.psum(jnp.dot(attn_low, w_out, preferred_element_type=jnp.float32), 'tp')]
    reduce_scatter x8 -> x0, waiting for transfers between devices: 463 us -> none  [the longest x1 125 us: shards(): lax.psum_scatter(grad_kv_all, 'blk', scatter_dimension=0, tiled=True)]
    pallas_call x0 -> x2, Pallas kernels: none -> 246 us  [the longest x1 241 us: kernel_shards(): pl.pallas_call(functools.partial(layer_kernel, dims), out_shape=shapes, i...]
    dot_general x28 -> x0, matrix products: 77.4 us -> none  [the longest x7 34.1 us: left_product(): lax.dot_general(left_side, right_side, (((0,), (0,)), ((), ())), preferre...]
    all_gather x1 -> x0, waiting for transfers between devices: 32.8 us -> none  [shards(): piece = lax.all_gather(kv_rows, 'blk', axis=0, tiled=True)]
    unnamed x1 -> x0, blocking collectives: 24.1 us -> none
    reduce_sum x9 -> x0, other arithmetic: 16.4 us -> none  [the longest x2 7.55 us: norm_back(): return (grad_values, jnp.sum(grad_in * normed, axis=0))]
  transfers between devices with their start and end apart: 12 -> 0, of which waited for: 12 -> 0; matrix products, arithmetic and copies ran while one was open for 5% -> 0% of each run, Pallas kernels for 0% -> 0%
where the time goes in v2:
time: 248 us; the launch traced here: 247 us
  Pallas kernels  246 us (99%)
    pallas_call x1, Pallas kernels, kernel_shards(): pl.pallas_call(functools.partial(layer_kernel, dims), out_shape=shapes, i...  241 us
    pallas_call x1, Pallas kernels, kernel_shards(): pl.pallas_call(functools.partial(hand_over, len(shapes)), out_shape=shape...  5.21 us

profile of v2, /device:TPU:0, one launch (start us, length us, event | category | flops | bytes accessed | tf_op | source)
XLA Modules:
  0.0 247.3 jit_solution(8686447980694576704)
XLA Ops:
  0.6 241.2 %shard_map.203 = (bf16[512,1536]{1,0:T(8,128)(2,1)}, bf16[512,1536]{1,0:T(8,128)(2,1)}, f32[192,384]{1,0:T(8,128)}, f32[192,192]{1,0:T(8,128)}, f32[192,192]{1,0...) custom-call(s32[5]{0:T(128)} %len_ref.1, ...), custom_call_target="tpu_custom_call" | custom-call | tf_op jit(solution)/shard_map/pallas_call | solution.py:1152
  241.9 5.2 %shard_map.204 = (bf16[512,1536]{1,0:T(8,128)(2,1)}, bf16[512,1536]{1,0:T(8,128)(2,1)}, f32[192,384]{1,0:T(8,128)}, f32[192,192]{1,0:T(8,128)}, f32[192,192]{1,0...) custom-call(bf16[512,1536]{1,0:T(8,128)(2,1)} %get-tuple-element.33., ...), custom_call_target="tpu_custom_call" | custom-call | tf_op jit(solution)/shard_map/pallas_call | solution.py:1181

commit v3 on v2

--- a/solution.py
+++ b/solution.py
@@ -422,20 +422,28 @@
         def _():
             self.copy(2, p).wait_recv()
 
-    def drain(self, pieces):
-        def one(p, carry):
-            @pl.when(self.me.outer)
-            def _():
+    def drain_outer(self, pieces):
+        @pl.when(self.me.outer)
+        def _():
+            def one(p, carry):
                 self.copy(0, p).wait_send()
-
-            @pl.when(self.me.inner)
-            def _():
+                return carry
+
+            lax.fori_loop(0, pieces, one, 0)
+
+    def drain_inner(self, pieces):
+        @pl.when(self.me.inner)
+        def _():
+            def one(p, carry):
                 self.copy(1, p).wait_send()
                 self.copy(2, p).wait_send()
-
-            return carry
-
-        lax.fori_loop(0, pieces, one, 0)
+                return carry
+
+            lax.fori_loop(0, pieces, one, 0)
+
+    def drain(self, pieces):
+        self.drain_outer(pieces)
+        self.drain_inner(pieces)
 
 
 class LineGather:
@@ -498,8 +506,8 @@
 
 
 class BlockSum:
-    def __init__(self, me, make, outs, held, mates, chips, sems):
-        self.me, self.make, self.outs = me, make, outs
+    def __init__(self, me, make, outs, held, mates, chips, sems, spare):
+        self.me, self.make, self.outs, self.spare = me, make, outs, spare
         self.held, self.mates, self.chips, self.sems = held, mates, chips, sems
 
     def to_mate(self, k):
@@ -521,18 +529,22 @@
             self.to_mate(k - 2).wait_send()
         held = self.held(k % 2)
         even = me.core == 0
-        for (lo, hi, value), out in zip(self.make(me.chip_at(k)), self.outs):
+        for (lo, hi, value), out, spare in zip(self.make(me.chip_at(k)), self.outs, self.spare):
             half = value.shape[0] // 2
             low, high = value[:half], value[half:]
             held[:, lo:hi] = jnp.where(even, high, low).astype(BF16)
-            out[...] = jnp.where(even, low, high)
+            if k % 2 == 0:
+                spare[...] = jnp.where(even, low, high).astype(BF16)
+            else:
+                out[...] = jnp.where(even, low, high)
         self.to_mate(k).start()
 
     def merge(self, k, spans):
         self.to_mate(k).wait_recv()
         mates = self.mates(k)
-        for (lo, hi), out in zip(spans, self.outs):
-            total = out[...] + mates[:, lo:hi].astype(F32)
+        for (lo, hi), out, spare in zip(spans, self.outs, self.spare):
+            own = spare[...].astype(F32) if k % 2 == 0 else out[...]
+            total = own + mates[:, lo:hi].astype(F32)
             if k < 3:
                 mates[:, lo:hi] = total.astype(BF16)
             else:
@@ -590,7 +602,7 @@
     p2, a2, b2, p3, a3, b3, dbr, dot_ref, dq, acc, low_t, dqr, dkvr,
     kv_mates, kv_chips, held_a, held_b, chips_b, held_c, mates_c, chips_c, total_c,
     turns, starts, m_ref, l_ref, lse, delta, gain, gain_in,
-    load_sem, kv_sem, wo_sem, wo_mate_sem, at_sem, sem2, sem3, sem4, kvs_sem, rs_sem, gain_sem, out_sem,
+    load_sem, kv_sem, wo_sem, wo_plane_sem, wo_mate_sem, at_sem, sem2, sem3, sem4, kvs_sem, rs_sem, gain_sem, out_sem,
     mate_ready, chip_ready,
 ):
     rows, piece, chunk, share = dims["rows"], dims["piece"], dims["chunk"], dims["share"]
@@ -617,13 +629,72 @@
         pl.semaphore_signal(barrier, inc=1, device_id=(me.b, z), device_id_type=MESH)
     loads = {}
     for i, (name, source, target) in enumerate((
-        ("hid", hid_hbm, hid), ("wo", wo_hbm, wo.at[me.t]), ("wk", wk_hbm, wkv.at[0:kv_width]),
+        ("wo", wo_hbm, wo.at[me.t]), ("hid", hid_hbm, hid), ("wk", wk_hbm, wkv.at[0:kv_width]),
         ("wv", wv_hbm, wkv.at[kv_width : 2 * kv_width]), ("wq", wq_hbm, wq), ("wg", wg_hbm, wg),
         ("wu", wu_hbm, wu), ("og", og_hbm, og), ("wd", wd_hbm, wd),
     )):
         loads[name] = pltpu.make_async_copy(source, target, load_sem.at[i])
+    for name in ("wo", "hid", "wk", "wv"):
         loads[name].start()
 
+    attn_gain, mlp_gain = ag_ref[...].reshape(1, width), mg_ref[...].reshape(1, width)
+
+    def chunk_rows(c):
+        return pl.ds(pl.multiple_of(c * chunk, chunk), chunk)
+
+    def first_norm(c):
+        r = chunk_rows(c)
+        normed, _ = norm_rows(hid[r, :].astype(F32))
+        norm[r, :] = (normed * attn_gain).astype(BF16)
+
+    part = share // 4
+    my_half = pl.ds(pl.multiple_of(me.core * share, share), share)
+
+    def wo_rows(slot, p):
+        first = me.core * share + p * 2 * part + (me.x, me.y)[p] * part
+        return wo.at[slot, pl.ds(pl.multiple_of(first, part), part), :]
+
+    whole_wo = LineGather(me, wo_rows, wo_sem.at[0], wo_sem.at[1], last)
+
+    def wo_plane(way, hop, p):
+        ref = wo_rows(me.t - hop if way == 0 else me.t + hop, p)
+        return remote(
+            ref, ref, wo_plane_sem.at[0, p, way, hop - 1], wo_plane_sem.at[1, p, way, hop - 1],
+            me.slot(2 + 2 * p), me.t,
+        )
+
+    def wo_to_mate(way, hop):
+        ref = wo.at[me.t - hop if way == 0 else me.t + hop, my_half, :]
+        return remote(
+            ref, ref, wo_mate_sem.at[0, way, hop - 1], wo_mate_sem.at[1, way, hop - 1], me.mate, me.t
+        )
+
+    def each_wo(hops, action):
+        for hop in hops:
+            for way in (0, 1):
+
+                @pl.when(whole_wo.gets(way, hop))
+                def _(way=way, hop=hop):
+                    action(way, hop)
+
+    def wo_spread(way, hop):
+        for p in (0, 1):
+            wo_plane(way, hop, p).start()
+
+    def wo_lend(way, hop):
+        for p in (0, 1):
+            wo_plane(way, hop, p).wait_recv()
+        wo_to_mate(way, hop).start()
+
+    def wo_line(hop):
+        for p in (0, 1):
+            whole_wo.step(hop, p)
+
+    loads["wo"].wait()
+    pl.semaphore_wait(barrier, 9)
+    for p in (0, 1):
+        whole_wo.send(1, p)
+    loads["wq"].start()
     places = me.b * rows + lax.broadcasted_iota(jnp.int32, (1, rows), 1)
     start, end = jnp.zeros((1, rows), jnp.int32), jnp.int32(0)
     for k in range(n_docs):
@@ -635,33 +706,8 @@
     angle = freqs * (places - start).astype(F32)
     turns[0:HALF, :] = jnp.cos(angle)
     turns[HALF:HEAD_SIZE, :] = jnp.sin(angle)
-    attn_gain, mlp_gain = ag_ref[...].reshape(1, width), mg_ref[...].reshape(1, width)
-
-    def chunk_rows(c):
-        return pl.ds(pl.multiple_of(c * chunk, chunk), chunk)
-
-    def first_norm(c):
-        r = chunk_rows(c)
-        normed, _ = norm_rows(hid[r, :].astype(F32))
-        norm[r, :] = (normed * attn_gain).astype(BF16)
-
     loads["hid"].wait()
     each(first_norm, 0, n_chunks)
-    loads["wo"].wait()
-    pl.semaphore_wait(barrier, 9)
-
-    my_half = pl.ds(pl.multiple_of(me.core * share, share), share)
-    whole_wo = LineGather(me, lambda slot, p: wo.at[slot, my_half, :], wo_sem.at[0], wo_sem.at[1], last)
-
-    def wo_to_mate(way, hop):
-        slot = me.t - hop if way == 0 else me.t + hop
-        ref = wo.at[slot, my_half, :]
-        return remote(
-            ref, ref, wo_mate_sem.at[0, way, hop - 1], wo_mate_sem.at[1, way, hop - 1], me.mate, me.t
-        )
-
-    whole_wo.send(1, 0)
-
     loads["wk"].wait()
     loads["wv"].wait()
     both_t = dot_nt(wkv[...], norm[...])
@@ -678,6 +724,8 @@
 
     for s in (1, 2, 4):
         share_kv(s)
+    for name in ("wg", "wu", "og", "wd"):
+        loads[name].start()
     loads["wq"].wait()
     qt[...] = turn(dot_nn(norm[...], wq[...]).T, turns, 1.0).astype(BF16)
     m_ref[...] = jnp.full(m_ref.shape, neg_fill, F32)
@@ -696,9 +744,15 @@
         def _():
             kv_copy(slot, me.mate, s + 1).start()
 
-        @pl.when(s == 5)
-        def _():
-            whole_wo.step(1, 0, wo_to_mate)
+        for hop, turn_at in ((1, 2), (2, 3), (3, 5)):
+
+            @pl.when(s == turn_at)
+            def _(hop=hop):
+                wo_line(hop)
+
+        @pl.when(s == 6)
+        def _():
+            each_wo((1, 2, 3), wo_spread)
 
         @pl.when(slot <= me.b)
         def _():
@@ -722,7 +776,6 @@
         return carry
 
     lax.fori_loop(0, 8, attend, 0)
-    whole_wo.step(2, 0, wo_to_mate)
 
     line_attn = LineGather(
         me, lambda slot, p: attn.at[slot, chunk_rows(p), :], at_sem.at[0], at_sem.at[1], last
@@ -738,22 +791,26 @@
     lse[0:q_heads, :] = m_ref[0:q_heads, :] * scale2 + jnp.log2(l_ref[0:q_heads, :])
     for name in ("wg", "wu", "og", "wd"):
         loads[name].wait()
-    for hop in range(1, last + 1):
-        line_attn.step(hop, 0)
-    whole_wo.step(3, 0, wo_to_mate)
-    for hop in range(1, last + 1):
-        for way in (0, 1):
-
-            @pl.when(whole_wo.gets(way, hop))
-            def _(way=way, hop=hop):
-                wo_to_mate(way, hop).wait_recv()
+    line_attn.step(1, 0)
+    line_attn.step(2, 0)
+    each_wo((1, 2, 3), wo_lend)
+    line_attn.step(3, 0)
+    line_attn.step(1, 1)
+    each_wo((1, 2, 3), lambda way, hop: wo_to_mate(way, hop).wait_recv())
 
     back = LineSum(me, p2, a2, b2, sem2, piece)
-    forth = LineSum(me, p3, a3, b3, sem3, piece)
+    forth_rows = rows // 8
+    forth = LineSum(me, p3, a3, b3, sem3, forth_rows)
+    forth_pieces = 8
     adds_middle = (me.t == 1).astype(F32)
 
     def feed(c, carry):
         r = chunk_rows(c)
+
+        @pl.when(c < n_chunks - 2)
+        def _():
+            line_attn.send(1, c + 2)
+
         for n in range(0, width, 512):
             ns = slice(n, n + 512)
             total = hid[r, ns].astype(F32)
@@ -763,13 +820,9 @@
         normed, _ = norm_rows(mid[r, :])
         norm[r, :] = (normed * mlp_gain).astype(BF16)
 
-        @pl.when(c >= 1)
-        def _():
-            each(back.fold, (c - 1) * per, c * per)
-
         @pl.when(c < n_chunks - 1)
         def _():
-            line_attn.step(1, c + 1)
+            line_attn.step(2, c + 1)
 
         for n in range(0, hidden_units, 512):
             ns = slice(n, n + 512)
@@ -783,26 +836,26 @@
             du[r, ns] = (grad * silu).astype(BF16)
             if n == 0:
 
-                @pl.when(c < n_chunks - 1)
-                def _():
-                    line_attn.step(2, c + 1)
-
                 @pl.when(c < n_chunks - 2)
                 def _():
-                    line_attn.send(1, c + 2)
+                    line_attn.step(1, c + 2)
 
         for n in range(0, width, 512):
             ns = slice(n, n + 512)
             p2[r, ns] = (dot_nt(dg[r, :], wg[ns, :]) + dot_nt(du[r, :], wu[ns, :])).astype(BF16)
         each(back.give, c * per, (c + 1) * per)
 
-        @pl.when(c >= 1)
-        def _():
-            each(back.unfold, (c - 1) * per, c * per)
-
         @pl.when(c < n_chunks - 1)
         def _():
             line_attn.step(3, c + 1)
+
+        @pl.when(c >= 2)
+        def _():
+            each(back.fold, (c - 2) * per, (c - 1) * per)
+
+        @pl.when(c >= 3)
+        def _():
+            each(back.unfold, (c - 3) * per, (c - 2) * per)
 
         for n in range(0, width, 512):
             ns = slice(n, n + 512)
@@ -815,7 +868,6 @@
         pl.semaphore_signal(
             chip_ready, inc=1, device_id=(me.chip_at(k) * 2 + me.core, me.t), device_id_type=MESH
         )
-    each(forth.give, 0, n_pieces)
     pair = 2 * share
 
     def pair_columns(ref, chip):
@@ -827,10 +879,12 @@
     sum_gate = BlockSum(
         me, lambda m: [(0, hidden_units, dot_tn(pair_columns(norm, m), dg[...]))], [gg_ref],
         lambda k: held_a.at[0, k], slots(wg, 0, hidden_units), slots(wg, 4, hidden_units), rs_sem.at[0],
+        [slots(wg, 7, hidden_units)(0)],
     )
     sum_up = BlockSum(
         me, lambda m: [(0, hidden_units, dot_tn(pair_columns(norm, m), du[...]))], [gu_ref],
         lambda k: held_a.at[1, k], slots(wu, 0, hidden_units), slots(wu, 4, hidden_units), rs_sem.at[1],
+        [slots(wu, 7, hidden_units)(0)],
     )
     span_a = [(0, hidden_units)]
     pl.semaphore_wait(mate_ready, 1)
@@ -849,30 +903,47 @@
         mid[r, :] = found
         dbr[r, :] = found.astype(BF16)
 
-    sum_gate.lend(0)
-    sum_up.lend(0)
-    each(back.fold, n_pieces - per, n_pieces)
+    def fold_on(lo, hi):
+        def one(p, carry):
+            back.fold(p)
+            back.unfold(p - per)
+            return carry
+
+        lax.fori_loop(lo, hi, one, 0)
+
+    def lend_both(k):
+        sum_gate.lend(k)
+        sum_up.lend(k)
+
+    def merge_both(k):
+        sum_gate.merge(k, span_a)
+        sum_up.merge(k, span_a)
+
+    lend_both(0)
+    fold_on((n_chunks - 2) * per, (n_chunks - 2) * per + per // 2)
+    lend_both(1)
+    back.drain_outer(n_pieces)
+    each(forth.give, 0, forth_pieces)
+    fold_on((n_chunks - 2) * per + per // 2, (n_chunks - 1) * per)
     pl.semaphore_wait(chip_ready, 3)
-    sum_gate.merge(0, span_a)
-    sum_up.merge(0, span_a)
-    sum_gate.lend(1)
-    sum_up.lend(1)
+    merge_both(0)
+    fold_on((n_chunks - 1) * per, n_pieces - per // 2)
+    lend_both(2)
+    merge_both(1)
+    fold_on(n_pieces - per // 2, n_pieces)
+    merge_both(2)
     each(back.unfold, n_pieces - per, n_pieces)
-    sum_gate.merge(1, span_a)
-    sum_up.merge(1, span_a)
     each(middle_grad, 0, n_chunks - 1)
-    sum_gate.lend(2)
-    sum_up.lend(2)
     each(middle_grad, n_chunks - 1, n_chunks)
     dot_ref[...] = dot_nt(wo[me.t], dbr[...]).astype(BF16)
-    sum_gate.merge(2, span_a)
-    sum_up.merge(2, span_a)
     delta[...] = jnp.zeros(delta.shape, F32)
     for h in range(q_heads):
         qs, _, _ = heads_of(h, group)
         delta[h : h + 1, :] = jnp.sum(dot_ref[qs, :].astype(F32) * ot[qs, :], axis=0, keepdims=True)
     dq[...] = jnp.zeros(dq.shape, F32)
-    back.drain(n_pieces)
+    back.drain_inner(n_pieces)
+    ahead = 3
+    each(forth.fold, 0, ahead)
 
     for s in (1, 2, 4, 6):
 
@@ -902,11 +973,14 @@
         k, own = u // 2, u % 2
         chip = me.chip_at(k)
         slot = chip * 2 + (me.core + 1 - own) % 2
-        forth.fold(u)
-
-        @pl.when(u >= 1)
-        def _():
-            forth.unfold(u - 1)
+
+        @pl.when(u + ahead < forth_pieces)
+        def _():
+            forth.fold(u + ahead)
+
+        @pl.when(u >= 2)
+        def _():
+            forth.unfold(u - 2)
 
         @pl.when(slot <= me.b)
         def _():
@@ -945,7 +1019,6 @@
         return carry
 
     lax.fori_loop(0, 8, attend_back, 0)
-    forth.unfold(n_pieces - 1)
     low_t[0:q_width, :] = turn(dq[...] * SCORE_SCALE, turns, -1.0).astype(BF16)
     dqr[...] = low_t[0:q_width, :].T
 
@@ -954,11 +1027,6 @@
         normed, _ = norm_rows(hid[r, :].astype(F32))
         norm[r, :] = (normed * attn_gain).astype(BF16)
 
-    sum_gate.lend(3)
-    sum_up.lend(3)
-    each(first_norm_again, 0, n_chunks)
-    sum_gate.merge(3, span_a)
-    sum_up.merge(3, span_a)
 
     @pl.when(me.core == 0)
     def _():
@@ -976,9 +1044,7 @@
     low_t[q_width + kv_width :, :] = acc[kv_width : 2 * kv_width, :].astype(BF16)
     dkvr[...] = low_t[q_width:, :].T
 
-    each(forth.take, 0, n_pieces)
-    lo_save = pltpu.make_async_copy(a3, lo_out, out_sem.at[0])
-    lo_save.start()
+    each(forth.take, 0, 2)
     end_sum = LineSum(me, p2, a2, b2, sem4, piece)
 
     def input_part(c):
@@ -989,6 +1055,7 @@
         each(end_sum.give, c * per, (c + 1) * per)
 
     each(input_part, 0, n_chunks)
+    each(forth.unfold, forth_pieces - 2, forth_pieces)
 
     def make_b(m):
         yield 0, hidden_units, dot_tn(pair_columns(og, m), act[...])
@@ -1004,30 +1071,40 @@
     sum_b = BlockSum(
         me, make_b, [gd_ref, go_ref], lambda k: held_b.at[k], in_wd,
         lambda k: in_wd(4) if k == 0 else chips_b.at[k - 1], rs_sem.at[2],
+        [dg.at[0:share, :], du.at[0:share, 0:q_width]],
     )
     span_b = [(0, hidden_units), (hidden_units, width_b)]
     total_parts = [total_c.at[:, 0:q_width], total_c.at[:, q_width : q_width + 2 * kv_width]]
     sum_c = BlockSum(
         me, make_c, total_parts, lambda k: held_c.at[k], lambda k: mates_c.at[k], lambda k: chips_c.at[k],
         rs_sem.at[3],
+        [dg.at[share : 2 * share, 0:q_width], du.at[share : 2 * share, 0 : 2 * kv_width]],
     )
     span_c = [(0, q_width), (q_width, q_width + 2 * kv_width)]
-    work = []
+    work = [(functools.partial(lend_both, 3), functools.partial(merge_both, 3))]
     for sums, spans in ((sum_b, span_b), (sum_c, span_c)):
         for k in range(4):
-            work.append((sums, k, spans))
-    for p in range(n_pieces):
-        if p >= 1:
-            sums, k, spans = work[p - 1]
-            sums.merge(k, spans)
-        sums, k, spans = work[p]
-        sums.lend(k)
-        end_sum.fold(p)
-        if p >= 1:
-            end_sum.unfold(p - 1)
+            work.append((functools.partial(sums.lend, k), functools.partial(sums.merge, k, spans)))
+    done, late = 0, None
+    for i, (lend, merge) in enumerate(work):
+        if i == 1:
+            each(first_norm_again, 0, n_chunks)
+        lend()
+        upto = n_pieces * (i + 1) // len(work)
+        for p in range(done, upto):
+            end_sum.fold(p)
+            if p >= 1:
+                end_sum.unfold(p - 1)
+        done = upto
+        if late is not None:
+            late()
+        late = merge
     end_sum.unfold(n_pieces - 1)
-    sums, k, spans = work[n_pieces - 1]
-    sums.merge(k, spans)
+    late()
+
+    each(forth.take, 2, forth_pieces)
+    lo_save = pltpu.make_async_copy(a3, lo_out, out_sem.at[0])
+    lo_save.start()
 
     def input_rows(c):
         each(end_sum.take, c * per, (c + 1) * per)
@@ -1069,16 +1146,17 @@
 
     for s in range(1, 8):
         gain_copy(s).wait_send()
-    whole_wo.drain(0)
-    for hop in range(1, last + 1):
-        for way in (0, 1):
-
-            @pl.when(whole_wo.gets(way, hop))
-            def _(way=way, hop=hop):
-                wo_to_mate(way, hop).wait_send()
-
+    for p in (0, 1):
+        whole_wo.drain(p)
+
+    def wo_done(way, hop):
+        for p in (0, 1):
+            wo_plane(way, hop, p).wait_send()
+        wo_to_mate(way, hop).wait_send()
+
+    each_wo((1, 2, 3), wo_done)
     each(line_attn.drain, 0, n_chunks)
-    forth.drain(n_pieces)
+    forth.drain(forth_pieces)
     end_sum.drain(n_pieces)
     for sums in (sum_gate, sum_up, sum_b, sum_c):
         sums.drain()
@@ -1122,7 +1200,7 @@
     hidden_units = w_gate.shape[1]
     blocks, line_size = lax.axis_size("blk"), lax.axis_size("tp")
     share = width // blocks
-    piece, chunk = rows // 8, rows // 4
+    piece, chunk = rows // 16, rows // 4
     pieces, chunks = rows // piece, rows // chunk
     dims = dict(
         rows=rows, piece=piece, chunk=chunk, share=share, q_heads=q_width // HEAD_SIZE,
@@ -1167,7 +1245,8 @@
             low(2, share, width_c), low(4, share, width_c), low(3, share, width_c), full(share, width_c),
             full(HEAD_SIZE, rows), pltpu.VMEM((8, rows), jnp.int32), full(8, rows), full(8, rows), full(8, rows),
             full(8, rows), full(8, width), full(8, 8, width),
-            dma((9,)), dma((2, 8)), dma((2, 2, line_size - 1, 1)), dma((2, 2, line_size - 1)),
+            dma((9,)), dma((2, 8)), dma((2, 2, line_size - 1, 2)), dma((2, 2, 2, line_size - 1)),
+            dma((2, 2, line_size - 1)),
             dma((2, 2, line_size - 1, chunks)), dma((6, pieces)), dma((6, pieces)), dma((6, pieces)),
             dma((4, 4)), dma((4, 4, 4)), dma((2, 8)), dma((2,)), regular, regular,
         ],

time: 248 us -> 220 us (0.89)
  Pallas kernels: 246 us -> 217 us
    pallas_call x1, Pallas kernels: 241 us -> 211 us  [kernel_shards(): pl.pallas_call(functools.partial(layer_kernel, dims), out_shape=shapes, i...]
where the time goes in v3:
time: 220 us; the launch traced here: 217 us
  Pallas kernels  217 us (99%)
    pallas_call x1, Pallas kernels, kernel_shards(): pl.pallas_call(functools.partial(layer_kernel, dims), out_shape=shapes, i...  211 us
    pallas_call x1, Pallas kernels, kernel_shards(): pl.pallas_call(functools.partial(hand_over, len(shapes)), out_shape=shape...  5.21 us

profile of v3, /device:TPU:0, one launch (start us, length us, event | category | flops | bytes accessed | tf_op | source)
XLA Modules:
  0.0 217.4 jit_solution(691715927899226308)
XLA Ops:
  0.6 211.4 %shard_map.203 = (bf16[512,1536]{1,0:T(8,128)(2,1)}, bf16[512,1536]{1,0:T(8,128)(2,1)}, f32[192,384]{1,0:T(8,128)}, f32[192,192]{1,0:T(8,128)}, f32[192,192]{1,0...) custom-call(s32[5]{0:T(128)} %len_ref.1, ...), custom_call_target="tpu_custom_call" | custom-call | tf_op jit(solution)/shard_map/pallas_call | solution.py:1230
  212.1 5.2 %shard_map.204 = (bf16[512,1536]{1,0:T(8,128)(2,1)}, bf16[512,1536]{1,0:T(8,128)(2,1)}, f32[192,384]{1,0:T(8,128)}, f32[192,192]{1,0:T(8,128)}, f32[192,192]{1,0...) custom-call(bf16[512,1536]{1,0:T(8,128)(2,1)} %get-tuple-element.33., ...), custom_call_target="tpu_custom_call" | custom-call | tf_op jit(solution)/shard_map/pallas_call | solution.py:1260

commit v4 on v3

--- a/solution.py
+++ b/solution.py
@@ -690,10 +690,6 @@
         for p in (0, 1):
             whole_wo.step(hop, p)
 
-    loads["wo"].wait()
-    pl.semaphore_wait(barrier, 9)
-    for p in (0, 1):
-        whole_wo.send(1, p)
     loads["wq"].start()
     places = me.b * rows + lax.broadcasted_iota(jnp.int32, (1, rows), 1)
     start, end = jnp.zeros((1, rows), jnp.int32), jnp.int32(0)
@@ -714,6 +710,10 @@
     kv[me.b, 0:kv_width, :] = turn(both_t[0:kv_width], turns, 1.0).astype(BF16)
     kv[me.b, kv_width : 2 * kv_width, :] = both_t[kv_width : 2 * kv_width].astype(BF16)
 
+    loads["wo"].wait()
+    pl.semaphore_wait(barrier, 9)
+    for p in (0, 1):
+        whole_wo.send(1, p)
     def kv_copy(slot, target, n):
         return remote(kv.at[slot], kv.at[slot], kv_sem.at[0, n], kv_sem.at[1, n], target, me.t)
 
@@ -785,15 +785,14 @@
         ot[qs, :] = ot[qs, :] / l_ref[h : h + 1, :]
     for c in range(n_chunks):
         attn[me.t, c * chunk : (c + 1) * chunk, :] = ot[:, c * chunk : (c + 1) * chunk].T.astype(BF16)
-        if c < 2:
-            line_attn.send(1, c)
+        line_attn.send(1, c)
     lse[...] = jnp.zeros(lse.shape, F32)
     lse[0:q_heads, :] = m_ref[0:q_heads, :] * scale2 + jnp.log2(l_ref[0:q_heads, :])
     for name in ("wg", "wu", "og", "wd"):
         loads[name].wait()
     line_attn.step(1, 0)
+    each_wo((1, 2, 3), wo_lend)
     line_attn.step(2, 0)
-    each_wo((1, 2, 3), wo_lend)
     line_attn.step(3, 0)
     line_attn.step(1, 1)
     each_wo((1, 2, 3), lambda way, hop: wo_to_mate(way, hop).wait_recv())
@@ -806,10 +805,6 @@
 
     def feed(c, carry):
         r = chunk_rows(c)
-
-        @pl.when(c < n_chunks - 2)
-        def _():
-            line_attn.send(1, c + 2)
 
         for n in range(0, width, 512):
             ns = slice(n, n + 512)

time: 220 us -> 208 us (0.945)
  Pallas kernels: 217 us -> 206 us
    pallas_call x1, Pallas kernels: 211 us -> 200 us  [kernel_shards(): pl.pallas_call(functools.partial(layer_kernel, dims), out_shape=shapes, i...]
where the time goes in v4:
time: 208 us; the launch traced here: 206 us
  Pallas kernels  206 us (99%)
    pallas_call x1, Pallas kernels, kernel_shards(): pl.pallas_call(functools.partial(layer_kernel, dims), out_shape=shapes, i...  200 us
    pallas_call x1, Pallas kernels, kernel_shards(): pl.pallas_call(functools.partial(hand_over, len(shapes)), out_shape=shape...  5.21 us

profile of v4, /device:TPU:0, one launch (start us, length us, event | category | flops | bytes accessed | tf_op | source)
XLA Modules:
  0.0 206.4 jit_solution(961070073499324210)
XLA Ops:
  0.6 200.4 %shard_map.203 = (bf16[512,1536]{1,0:T(8,128)(2,1)}, bf16[512,1536]{1,0:T(8,128)(2,1)}, f32[192,384]{1,0:T(8,128)}, f32[192,192]{1,0:T(8,128)}, f32[192,192]{1,0...) custom-call(s32[5]{0:T(128)} %len_ref.1, ...), custom_call_target="tpu_custom_call" | custom-call | tf_op jit(solution)/shard_map/pallas_call | solution.py:1225
  201.0 5.2 %shard_map.204 = (bf16[512,1536]{1,0:T(8,128)(2,1)}, bf16[512,1536]{1,0:T(8,128)(2,1)}, f32[192,384]{1,0:T(8,128)}, f32[192,192]{1,0:T(8,128)}, f32[192,192]{1,0...) custom-call(bf16[512,1536]{1,0:T(8,128)(2,1)} %get-tuple-element.33., ...), custom_call_target="tpu_custom_call" | custom-call | tf_op jit(solution)/shard_map/pallas_call | solution.py:1255

commit v5 on v4

--- a/solution.py
+++ b/solution.py
@@ -1195,7 +1195,7 @@
     hidden_units = w_gate.shape[1]
     blocks, line_size = lax.axis_size("blk"), lax.axis_size("tp")
     share = width // blocks
-    piece, chunk = rows // 16, rows // 4
+    piece, chunk = rows // 8, rows // 4
     pieces, chunks = rows // piece, rows // chunk
     dims = dict(
         rows=rows, piece=piece, chunk=chunk, share=share, q_heads=q_width // HEAD_SIZE,

time: 208 us -> 206 us (level)
  no operation moved by 1% of the time
where the time goes in v5:
time: 206 us
  Pallas kernels  205 us (100%)
    pallas_call x1, Pallas kernels, kernel_shards(): pl.pallas_call(functools.partial(layer_kernel, dims), out_shape=shapes, i...  200 us
    pallas_call x1, Pallas kernels, kernel_shards(): pl.pallas_call(functools.partial(hand_over, len(shapes)), out_shape=shape...  5.21 us

profile of v5, /device:TPU:0, one launch (start us, length us, event | category | flops | bytes accessed | tf_op | source)
XLA Modules:
  0.0 205.8 jit_solution(3193847892000609133)
XLA Ops:
  0.6 199.7 %shard_map.203 = (bf16[512,1536]{1,0:T(8,128)(2,1)}, bf16[512,1536]{1,0:T(8,128)(2,1)}, f32[192,384]{1,0:T(8,128)}, f32[192,192]{1,0:T(8,128)}, f32[192,192]{1,0...) custom-call(s32[5]{0:T(128)} %len_ref.1, ...), custom_call_target="tpu_custom_call" | custom-call | tf_op jit(solution)/shard_map/pallas_call | solution.py:1225
  200.4 5.2 %shard_map.204 = (bf16[512,1536]{1,0:T(8,128)(2,1)}, bf16[512,1536]{1,0:T(8,128)(2,1)}, f32[192,384]{1,0:T(8,128)}, f32[192,192]{1,0:T(8,128)}, f32[192,192]{1,0...) custom-call(bf16[512,1536]{1,0:T(8,128)(2,1)} %get-tuple-element.33., ...), custom_call_target="tpu_custom_call" | custom-call | tf_op jit(solution)/shard_map/pallas_call | solution.py:1255

commit v6 on v5

--- a/solution.py
+++ b/solution.py
@@ -937,7 +937,7 @@
         delta[h : h + 1, :] = jnp.sum(dot_ref[qs, :].astype(F32) * ot[qs, :], axis=0, keepdims=True)
     dq[...] = jnp.zeros(dq.shape, F32)
     back.drain_inner(n_pieces)
-    ahead = 3
+    ahead = 2
     each(forth.fold, 0, ahead)
 
     for s in (1, 2, 4, 6):

time: 206 us -> 203 us (0.985)
  Pallas kernels: 205 us -> 202 us
    pallas_call x1, Pallas kernels: 200 us -> 197 us  [kernel_shards(): pl.pallas_call(functools.partial(layer_kernel, dims), out_shape=shapes, i...]
where the time goes in v6:
time: 203 us
  Pallas kernels  202 us (100%)
    pallas_call x1, Pallas kernels, kernel_shards(): pl.pallas_call(functools.partial(layer_kernel, dims), out_shape=shapes, i...  197 us
    pallas_call x1, Pallas kernels, kernel_shards(): pl.pallas_call(functools.partial(hand_over, len(shapes)), out_shape=shape...  5.21 us

profile of v6, /device:TPU:0, one launch (start us, length us, event | category | flops | bytes accessed | tf_op | source)
XLA Modules:
  0.0 202.6 jit_solution(12515687754117975337)
XLA Ops:
  0.6 196.5 %shard_map.203 = (bf16[512,1536]{1,0:T(8,128)(2,1)}, bf16[512,1536]{1,0:T(8,128)(2,1)}, f32[192,384]{1,0:T(8,128)}, f32[192,192]{1,0:T(8,128)}, f32[192,192]{1,0...) custom-call(s32[5]{0:T(128)} %len_ref.1, ...), custom_call_target="tpu_custom_call" | custom-call | tf_op jit(solution)/shard_map/pallas_call | solution.py:1225
  197.2 5.2 %shard_map.204 = (bf16[512,1536]{1,0:T(8,128)(2,1)}, bf16[512,1536]{1,0:T(8,128)(2,1)}, f32[192,384]{1,0:T(8,128)}, f32[192,192]{1,0:T(8,128)}, f32[192,192]{1,0...) custom-call(bf16[512,1536]{1,0:T(8,128)(2,1)} %get-tuple-element.33., ...), custom_call_target="tpu_custom_call" | custom-call | tf_op jit(solution)/shard_map/pallas_call | solution.py:1255
